TPU v7x, 32 devices: a whole 2x2x4 slice. The times are simulated.
32 devices in a mesh: gz: 8 (over y, x, core), gy: 4 (over z).
Axes of the slice: x: 2, y: 2, z: 4, core: 2. Of those that a mesh axis runs over, the one named last changes fastest.
Arguments:
- potential: float32 [24, 512, 2048], P('gz', 'gy'), may hold values from -3 to 301
- external: float32 [24, 512, 2048], P('gz', 'gy'), may hold values from -4 to 4
Outputs:
- dual_field: float32 [24, 512, 2048], P('gz', 'gy')
- density_log: float32 [24, 512, 2048], P('gz', 'gy')
All inputs are finite; a program needn't handle non-finite values.
Results may differ from a plain program's by a relative error of at most 0.0001.
Values sent between devices are 32-bit elements; how exact they have to be, the bound alone decides.
No kernel may reach another device: no remote copies, remote signals or barrier semaphores. Data moves between devices by JAX's collectives and lax.ppermute only.
A program may use at most 128 MiB of HBM per device.

v0:
```python
import jax
import jax.numpy as jnp
from jax import lax
from jax.sharding import PartitionSpec as P

RADIUS = 128


HIGHEST = lax.Precision.HIGHEST


def padded_2(cells, sides, width):
    for axis, dim in sides:
        count = lax.axis_size(axis)
        ends = count - 1
        head = lax.slice_in_dim(cells, 0, width, axis=dim)
        tail = lax.slice_in_dim(cells, cells.shape[dim] - width, cells.shape[dim], axis=dim)
        cells = jnp.concatenate(
            [
                lax.ppermute(tail, axis, [(i, (i + 1) % count) for i in range(ends)]),
                cells,
                lax.ppermute(head, axis, [((i + 1) % count, i) for i in range(ends)]),
            ],
            axis=dim,
        )
    return cells


def log_kernel(row_count, col_count, offset, radius):
    in_index = lax.broadcasted_iota(jnp.int32, (row_count, col_count), 0)
    out_index = lax.broadcasted_iota(jnp.int32, (row_count, col_count), 1)
    apart = in_index - offset - out_index
    distance = apart.astype(jnp.float32)
    inside = jnp.abs(apart) <= radius
    return jnp.where(inside, jnp.exp(-2.0 * distance * distance / float(radius * radius)), 0.0)


def along_last(source, radius):
    leading = source.shape[:-1]
    length = source.shape[-1]
    block_size = 2 * radius
    block_count = length // block_size
    border = jnp.full(leading + (radius,), -jnp.inf, jnp.float32)
    padded = jnp.concatenate([border, source, border], axis=-1)
    pieces = padded.reshape(leading + (block_count + 1, block_size))
    window = jnp.concatenate([pieces[..., :-1, :], pieces[..., 1:, :]], axis=-1)
    highest_value = jnp.max(window, axis=-1, keepdims=True)
    weights = jnp.exp(window - highest_value)
    kernel_table = log_kernel(2 * block_size, block_size, radius, radius)
    summed = jnp.einsum("...w,wo->...o", weights, kernel_table, precision=HIGHEST)
    return (jnp.log(summed) + highest_value).reshape(leading + (length,))


def along_middle(extended, own_rows, radius):
    highest_value = jnp.max(extended, axis=1, keepdims=True)
    weights = jnp.exp(extended - highest_value)
    kernel_table = log_kernel(own_rows + 2 * radius, own_rows, radius, radius)
    summed = jnp.einsum("zwx,wo->zox", weights, kernel_table, precision=HIGHEST)
    return jnp.log(summed) + highest_value


def along_first(source, radius):
    length = source.shape[0]
    highest_value = jnp.max(source, axis=0, keepdims=True)
    weights = jnp.exp(source - highest_value)
    kernel_table = log_kernel(length, length, 0, radius)
    summed = jnp.einsum("wyx,wo->oyx", weights, kernel_table, precision=HIGHEST)
    return jnp.log(summed) + highest_value


def proximal(logs, outer_field):
    shifted = logs - 0.5 * outer_field
    softer = jnp.maximum(shifted, 0.0) + jnp.log1p(jnp.exp(-jnp.abs(shifted)))
    log_level = jnp.log1p(softer)
    for newton_step in range(2):
        exp_level = jnp.exp(log_level)
        log_level = log_level - (log_level + exp_level - shifted) / (1.0 + exp_level)
    return (log_level - logs, log_level)


def local(potential, external):
    depth = RADIUS
    position = lax.axis_index("gy")
    devices = lax.axis_size("gy")
    own_rows = potential.shape[1]
    row_index = lax.broadcasted_iota(jnp.int32, (1, own_rows + 2 * depth, 1), 1)
    outside = (row_index < depth) & (position == 0) | (row_index >= own_rows + depth) & (
        position == devices - 1
    )
    along_x = along_last(potential, depth)
    extended = padded_2(along_x, (("gy", 1),), depth)
    extended = jnp.where(outside, -jnp.inf, extended)
    along_y = along_middle(extended, own_rows, depth)
    pencil_logs, pencil_outer = (
        lax.all_to_all(along_y, "gz", split_axis=1, concat_axis=0, tiled=True),
        lax.all_to_all(external, "gz", split_axis=1, concat_axis=0, tiled=True),
    )
    along_z = along_first(pencil_logs, depth)
    dual_part, density_part = proximal(along_z, pencil_outer)
    slab_dual, slab_density = (
        lax.all_to_all(dual_part, "gz", split_axis=0, concat_axis=1, tiled=True),
        lax.all_to_all(density_part, "gz", split_axis=0, concat_axis=1, tiled=True),
    )
    return (slab_dual, slab_density)


def solution(mesh):
    return jax.shard_map(
        local,
        mesh=mesh,
        in_specs=(P("gz", "gy", None), P("gz", "gy", None)),
        out_specs=(P("gz", "gy", None), P("gz", "gy", None)),
        check_vma=False,
    )
```

profile of v0, /device:TPU:0, one launch (start us, length us, event | category | flops | bytes accessed | tf_op | source)
XLA Modules:
  0.0 275.2 jit_solution(5257286183051829546)
XLA Ops:
  0.6 2.4 copy.45
  4.1 12.3 %log_add_fusion.1 = f32[3,128,8,256]{3,1,2,0:T(8,128)} fusion(f32[3,128,8,256]{1,3,2,0:T(8,128)S(1)} %get-tuple-element.6, f32[3,128,8,256]{1,3,2,0:T(8,128)S(1)} %get-tuple-element.7, f32[3,128,8]{1,2,0:T(8,128)S(1)} %reduce_max.40, s32[512]{0:T(512)S(1)} %iota_add_fusion), kind=kOutput, calls=%fused_computation.31 | convolution fusion | flops 4836818944 | bytes 9451520 | tf_op jit(solution)/shard_map/...w,wo->...o/dot_general | solution.py:50
  16.4 2.4 copy.47
  20.1 7.3 %collective-permute-start = (f32[3,128,2048]{1,2,0:T(8,128)S(1)}, f32[3,128,2048]{1,2,0:T(8,128)}, u32[]{:S(2)}, u32[]{:S(2)}) collective-permute-start(f32[3,128,2048]{1,2,0:T(8,128)S(1)} %bitcast.41), channel_id=1, source_target_pairs={{0,1},{1,2},{2,3},{4,5},{5,6},{6,7},{8,9},{9,10},{10,11},{12,13},{... | collective-permute-start | bytes 9437192 | tf_op jit(solution)/shard_map/ppermute | solution.py:20
  27.4 6.0 %copy.53 = f32[3,128,2048]{2,0,1:T(4,128)} copy(f32[3,128,2048]{2,1,0:T(8,128)} %param.3) | data formatting | bytes 6291456 | tf_op args[1]
  33.4 4.5 %all-to-all-start.1 = ((f32[3,128,2048]{2,0,1:T(4,128)}), f32[3,128,2048]{2,0,1:T(4,128)}, u32[]{:S(2)}, u32[]{:S(2)}) async-start(f32[3,128,2048]{2,0,1:T(4,128)} %copy.53), calls=%async_computation.1 | async-start | bytes 8388608 | tf_op jit(solution)/shard_map/all_to_all | solution.py:96
  38.0 53.9 %collective-permute-done.1 = f32[3,128,2048]{1,2,0:T(8,128)} collective-permute-done((f32[3,128,2048]{1,2,0:T(8,128)S(1)}, f32[3,128,2048]{1,2,0:T(8,128)}, u32[]{:S(2)}, u32[]{:S(2)}) %collective-permute-start.1) | collective-permute-done | bytes 3145760 | tf_op jit(solution)/shard_map/ppermute | solution.py:22
  93.0 3.3 %fusion.8 = f32[3,2048]{1,0:T(4,128)S(1)} fusion(f32[3,128,2048]{1,2,0:T(8,128)} %collective-permute-done.1, f32[3,128,2048]{1,2,0:T(8,128)S(1)} %bitcast.42, f32[3,128,2048]{1,2,0:T(8,128)} %collective-permute-done, pred[384]{0:T(512)(128)(4,1)S(1)} %fusion.71), kind=kLoop, calls=%fused_computation.9 | loop fusion | flops 9431040 | bytes 9462144 | tf_op jit(solution)/shard_map/reduce_max | solution.py:55
  96.3 13.1 %add_bitcast_fusion = f32[3,128,2048]{2,1,0:T(8,128)S(1)} fusion(f32[3,2048]{1,0:T(4,128)S(1)} %fusion.8, f32[3,128,2048]{1,2,0:T(8,128)} %collective-permute-done.1, f32[3,128,2048]{1,2,0:T(8,128)S(1)} %bitcast.43, f32[3,128,2048]{1,2,0:T(8,128)} %collective-permute-done, pred[384]{0:T(512)(128)(4,1)S(1)} %fusion.71, s32[384]{0:T(512)S(1)} %iota_add_fusion.1), kind=kOutput, calls=%fused_computation.30 | convolution fusion | flops 3634495488 | bytes 12609408 | tf_op jit(solution)/shard_map/zwx,wo->zox/dot_general | solution.py:58
  109.5 4.1 %copy.49 = f32[3,128,2048]{2,0,1:T(4,128)} copy(f32[3,128,2048]{2,1,0:T(8,128)S(1)} %add_bitcast_fusion) | data formatting | bytes 6291456 | tf_op jit(solution)/shard_map/add | solution.py:59
  113.6 4.8 %all-to-all-start = ((f32[3,128,2048]{2,0,1:T(4,128)}), f32[3,128,2048]{2,0,1:T(4,128)}, u32[]{:S(2)}, u32[]{:S(2)}) async-start(f32[3,128,2048]{2,0,1:T(4,128)} %copy.49), calls=%async_computation | async-start | bytes 8388608 | tf_op jit(solution)/shard_map/all_to_all | solution.py:95
  118.4 4.2 %copy_multiply_fusion = f32[3,128,2048]{2,1,0:T(8,128)S(1)} fusion(f32[3,128,2048]{2,0,1:T(4,128)} %all-to-all-done.1), kind=kLoop, calls=%fused_computation.25 | loop fusion | flops 786432 | bytes 6291456 | tf_op jit(solution)/shard_map/mul | solution.py:72
  122.6 2.0 copy.55
  124.6 42.7 %all-to-all-done = f32[3,128,2048]{2,0,1:T(4,128)} async-done(((f32[3,128,2048]{2,0,1:T(4,128)}), f32[3,128,2048]{2,0,1:T(4,128)}, u32[]{:S(2)}, u32[]{:S(2)}) %all-to-all-start) | async-done | bytes 3145760 | tf_op jit(solution)/shard_map/all_to_all | solution.py:95
  167.3 4.0 %copy.50 = f32[3,128,2048]{2,1,0:T(8,128)S(1)} copy(f32[3,128,2048]{2,0,1:T(4,128)} %all-to-all-done) | data formatting | bytes 6291456 | tf_op jit(solution)/shard_map/all_to_all | solution.py:95
  173.4 10.6 %fusion.87 = (f32[24,16,2048]{2,0,1:T(8,128)S(1)}, f32[24,16,2048]{2,0,1:T(8,128)}) fusion(f32[24,16,2048]{2,1,0:T(8,128)S(1)} %bitcast.44, f32[16,2048]{1,0:T(8,128)S(1)} %reduce_max.42, f32[24,16,2048]{2,1,0:T(8,128)S(1)} %bitcast.46), kind=kOutput, calls=%fused_computation.99 | convolution fusion | flops 240652800 | bytes 12713984 | tf_op jit(solution)/shard_map/wyx,wo->oyx/dot_general | solution.py:67
  184.0 3.5 %copy.57 = f32[24,16,2048]{2,1,0:T(8,128)} copy(f32[24,16,2048]{2,0,1:T(8,128)S(1)} %get-tuple-element.4) | data formatting | bytes 6291456 | tf_op jit(solution)/shard_map/sub | solution.py:78
  187.5 3.9 %all-to-all-start.2 = ((f32[24,16,2048]{2,1,0:T(8,128)}), f32[24,16,2048]{2,1,0:T(8,128)S(1)}, u32[]{:S(2)}, u32[]{:S(2)}) async-start(f32[24,16,2048]{2,1,0:T(8,128)} %copy.57), calls=%async_computation.2 | async-start | bytes 6291456 | tf_op jit(solution)/shard_map/all_to_all | solution.py:101
  191.4 5.4 %copy.59 = f32[24,16,2048]{2,1,0:T(8,128)} copy(f32[24,16,2048]{2,0,1:T(8,128)} %get-tuple-element.5) | data formatting | bytes 6291456 | tf_op jit(solution)/shard_map/sub | solution.py:77
  196.8 32.2 %all-to-all-done.2 = f32[24,16,2048]{2,1,0:T(8,128)S(1)} async-done(((f32[24,16,2048]{2,1,0:T(8,128)}), f32[24,16,2048]{2,1,0:T(8,128)S(1)}, u32[]{:S(2)}, u32[]{:S(2)}) %all-to-all-start.2) | async-done | bytes 3145760 | tf_op jit(solution)/shard_map/all_to_all | solution.py:101
  229.0 4.4 %all-to-all-start.3 = ((f32[24,16,2048]{2,1,0:T(8,128)}), f32[24,16,2048]{2,1,0:T(8,128)}, u32[]{:S(2)}, u32[]{:S(2)}) async-start(f32[24,16,2048]{2,1,0:T(8,128)} %copy.59), calls=%async_computation.3 | async-start | bytes 6291456 | tf_op jit(solution)/shard_map/all_to_all | solution.py:102
  233.4 1.9 copy.58
  235.3 36.0 %all-to-all-done.3 = f32[24,16,2048]{2,1,0:T(8,128)} async-done(((f32[24,16,2048]{2,1,0:T(8,128)}), f32[24,16,2048]{2,1,0:T(8,128)}, u32[]{:S(2)}, u32[]{:S(2)}) %all-to-all-start.3) | async-done | bytes 3145760 | tf_op jit(solution)/shard_map/all_to_all | solution.py:102
  271.3 3.9 %copy.60 = f32[3,8,16,2048]{3,2,1,0:T(8,128)} copy(f32[3,8,16,2048]{3,2,0,1:T(8,128)} %bitcast.18) | data formatting | bytes 6291456 | tf_op jit(solution)/shard_map/all_to_all | solution.py:102
  (14 shorter events, 5.5 us)
Async XLA Ops:
  18.8 73.1 %collective-permute-start.1 = (f32[3,128,2048]{1,2,0:T(8,128)S(1)}, f32[3,128,2048]{1,2,0:T(8,128)}, u32[]{:S(2)}, u32[]{:S(2)}) collective-permute-start(f32[3,128,2048]{1,2,0:T(8,128)S(1)} %bitcast.40), channel_id=1, source_target_pairs={{1,0},{2,1},{3,2},{5,4},{6,5},{7,6},{9,8},{10,9},{11,10},{13,12},{... | collective-permute-start | bytes 9437192 | tf_op jit(solution)/shard_map/ppermute | solution.py:22
  20.1 72.9 %collective-permute-start = (f32[3,128,2048]{1,2,0:T(8,128)S(1)}, f32[3,128,2048]{1,2,0:T(8,128)}, u32[]{:S(2)}, u32[]{:S(2)}) collective-permute-start(f32[3,128,2048]{1,2,0:T(8,128)S(1)} %bitcast.41), channel_id=1, source_target_pairs={{0,1},{1,2},{2,3},{4,5},{5,6},{6,7},{8,9},{9,10},{10,11},{12,13},{... | collective-permute-start | bytes 9437192 | tf_op jit(solution)/shard_map/ppermute | solution.py:20
  33.4 80.2 %all-to-all-start.1 = ((f32[3,128,2048]{2,0,1:T(4,128)}), f32[3,128,2048]{2,0,1:T(4,128)}, u32[]{:S(2)}, u32[]{:S(2)}) async-start(f32[3,128,2048]{2,0,1:T(4,128)} %copy.53), calls=%async_computation.1 | async-start | bytes 8388608 | tf_op jit(solution)/shard_map/all_to_all | solution.py:96
  113.6 53.7 %all-to-all-start = ((f32[3,128,2048]{2,0,1:T(4,128)}), f32[3,128,2048]{2,0,1:T(4,128)}, u32[]{:S(2)}, u32[]{:S(2)}) async-start(f32[3,128,2048]{2,0,1:T(4,128)} %copy.49), calls=%async_computation | async-start | bytes 8388608 | tf_op jit(solution)/shard_map/all_to_all | solution.py:95
  171.5 1.9 copy-start
  187.5 41.5 %all-to-all-start.2 = ((f32[24,16,2048]{2,1,0:T(8,128)}), f32[24,16,2048]{2,1,0:T(8,128)S(1)}, u32[]{:S(2)}, u32[]{:S(2)}) async-start(f32[24,16,2048]{2,1,0:T(8,128)} %copy.57), calls=%async_computation.2 | async-start | bytes 6291456 | tf_op jit(solution)/shard_map/all_to_all | solution.py:101
  229.0 42.3 %all-to-all-start.3 = ((f32[24,16,2048]{2,1,0:T(8,128)}), f32[24,16,2048]{2,1,0:T(8,128)}, u32[]{:S(2)}, u32[]{:S(2)}) async-start(f32[24,16,2048]{2,1,0:T(8,128)} %copy.59), calls=%async_computation.3 | async-start | bytes 6291456 | tf_op jit(solution)/shard_map/all_to_all | solution.py:102
where the time goes:
time: 277 us; the launch traced here: 275 us
  waiting for transfers between devices  166 us (60%)
  local copies, waits for them, and re-layouts  37.4 us (14%)
  matrix products  36.1 us (13%)
  starting transfers between devices  26.3 us (9%)
  other arithmetic  8.76 us (3%)
    ppermute x1, waiting for transfers between devices, padded_2(): lax.ppermute(head, axis, [((i + 1) % count, i) for i in range(ends)])  53.9 us
    all_to_all x1, waiting for transfers between devices, local(): lax.all_to_all(along_y, 'gz', split_axis=1, concat_axis=0, tiled=True)  42.7 us
    all_to_all x1, waiting for transfers between devices, local(): lax.all_to_all(density_part, 'gz', split_axis=0, concat_axis=1, tiled=True)  36 us
    all_to_all x1, waiting for transfers between devices, local(): lax.all_to_all(dual_part, 'gz', split_axis=0, concat_axis=1, tiled=True)  32.2 us
    dot_general x1, matrix products, along_middle(): summed = jnp.einsum('zwx,wo->zox', weights, kernel_table, precision=HIGHEST)  13.1 us
    dot_general x1, matrix products, along_last(): jnp.einsum('...w,wo->...o', weights, kernel_table, precision=HIGHEST)  12.3 us
    dot_general x1, matrix products, along_first(): summed = jnp.einsum('wyx,wo->oyx', weights, kernel_table, precision=HIGHEST)  10.6 us
    unnamed x4, local copies, waits for them, and re-layouts  10 us
  transfers between devices with their start and end apart: 6, of which 5 were waited for; matrix products, arithmetic and copies ran while one was open for 15% of the time, Pallas kernels for 0%

commit v1 on v0

v1 whole, which is shorter than its diff:
```python
import functools

import jax
import jax.numpy as jnp
import ml_dtypes
import numpy as np
from jax import lax
from jax.experimental import pallas as pl
from jax.experimental.pallas import tpu as pltpu
from jax.sharding import PartitionSpec as P

RADIUS = 128
BLOCK = 2 * RADIUS
LOWEST = -1e30

HIGHEST = lax.Precision.HIGHEST


def gauss(apart):
    apart = np.asarray(apart, np.float64)
    table = np.exp(-2.0 * apart * apart / float(RADIUS * RADIUS))
    return np.where(np.abs(apart) <= RADIUS, table, 0.0)


def two_terms(table):
    high = table.astype(ml_dtypes.bfloat16)
    low = (table - high.astype(np.float64)).astype(ml_dtypes.bfloat16)
    return high, low


def x_tables():
    table = gauss(np.arange(2 * BLOCK)[:, None] - RADIUS - np.arange(BLOCK)[None, :])
    return two_terms(table)


def y_table(rows):
    table = gauss(np.arange(rows + 2 * RADIUS)[None, :] - RADIUS - np.arange(rows)[:, None])
    return np.concatenate(two_terms(table), axis=0)


def split(weights):
    high = weights.astype(jnp.bfloat16)
    low = (weights - high.astype(jnp.float32)).astype(jnp.bfloat16)
    return high, low


def dot(a, b):
    return jnp.dot(a, b, preferred_element_type=jnp.float32)


def x_window(window, high_table, low_table):
    highest_value = jnp.max(window, axis=-1, keepdims=True)
    high, low = split(jnp.exp(window - highest_value))
    summed = dot(high, high_table) + (dot(low, high_table) + dot(high, low_table))
    return jnp.log(summed) + highest_value


def y_window(window, table):
    rows = table.shape[0] // 2
    highest_value = jnp.max(window, axis=0, keepdims=True)
    high, low = split(jnp.exp(window - highest_value))
    both = dot(table, high)
    summed = both[:rows] + (both[rows:] + dot(table[:rows], low))
    return jnp.log(summed) + highest_value


def proximal(logs, outer_field):
    shifted = logs - 0.5 * outer_field
    softer = jnp.maximum(shifted, 0.0) + jnp.log(1.0 + jnp.exp(-jnp.abs(shifted)))
    log_level = jnp.log(1.0 + softer)
    for newton_step in range(2):
        exp_level = jnp.exp(log_level)
        log_level = log_level - (log_level + exp_level - shifted) / (1.0 + exp_level)
    return log_level - logs, log_level


def slot_rows(place, slot, rows):
    return pl.ds(pl.multiple_of(lax.bitwise_xor(place, slot) * rows, rows), rows)


def params():
    return pltpu.CompilerParams(vmem_limit_bytes=48 * 1024 * 1024)


def cost(flops, count, transcendentals):
    return pl.CostEstimate(flops=int(flops), bytes_accessed=int(4 * count), transcendentals=int(transcendentals))


def x_kernel(first, last, slots, width, meta, *refs):
    refs = list(refs)
    main = refs.pop(0)
    left = None if first else refs.pop(0)
    right = None if last else refs.pop(0)
    high_ref, low_ref = refs.pop(0), refs.pop(0)
    outs = refs
    rows = main.shape[1]
    if slots:
        held = outs.pop()
    high_table, low_table = high_ref[...], low_ref[...]
    for j in range(width // BLOCK):
        begin, end = j * BLOCK - RADIUS, (j + 1) * BLOCK + RADIUS
        pieces = [main[0, :, max(begin, 0):min(end, width)]]
        table_from, table_to = 0, 2 * BLOCK
        if begin < 0:
            if first:
                table_from = RADIUS
            else:
                pieces.insert(0, left[0])
        if end > width:
            if last:
                table_to = 2 * BLOCK - RADIUS
            else:
                pieces.append(right[0])
        window = jnp.concatenate(pieces, axis=-1) if len(pieces) > 1 else pieces[0]
        result = x_window(window, high_table[table_from:table_to], low_table[table_from:table_to])
        columns = pl.ds(j * BLOCK, BLOCK)
        if slots:
            held[:, columns] = result
        else:
            outs[0][0, :, columns] = result
    if slots:
        for slot, out in enumerate(outs):
            out[0] = held[slot_rows(meta[0], slot, rows // slots), :]


def along_x(potential, meta, start, width, slots):
    depth, rows, length = potential.shape
    first, last = start == 0, start + width == length
    specs = [pl.BlockSpec((1, rows, width), lambda z, m: (z, 0, start // width))]
    if not first:
        specs.append(pl.BlockSpec((1, rows, RADIUS), lambda z, m: (z, 0, start // RADIUS - 1)))
    if not last:
        specs.append(pl.BlockSpec((1, rows, RADIUS), lambda z, m: (z, 0, (start + width) // RADIUS)))
    operands = [potential] * len(specs)
    for table in x_tables():
        specs.append(pl.BlockSpec(table.shape, lambda z, m: (0, 0)))
        operands.append(jnp.asarray(table))
    if slots:
        part = rows // slots
        outs = [jax.ShapeDtypeStruct((depth, part, width), jnp.float32)] * slots
        out_specs = [pl.BlockSpec((1, part, width), lambda z, m: (z, 0, 0))] * slots
        scratch = [pltpu.VMEM((rows, width), jnp.float32)]
    else:
        outs = jax.ShapeDtypeStruct((depth, rows, width), jnp.float32)
        out_specs = pl.BlockSpec((1, rows, width), lambda z, m: (z, 0, 0))
        scratch = []
    count = depth * rows * width
    return pl.pallas_call(
        functools.partial(x_kernel, first, last, slots, width),
        grid_spec=pltpu.PrefetchScalarGridSpec(
            num_scalar_prefetch=1, grid=(depth,), in_specs=specs, out_specs=out_specs, scratch_shapes=scratch
        ),
        out_shape=outs,
        compiler_params=params(),
        cost_estimate=cost(3 * 2 * 512 * count, 2 * count, 3 * count),
        name="along_x",
    )(meta, *operands)


def extended(meta, up, own, down):
    above = jnp.where(meta[1] == 1, -jnp.inf, up[0])
    below = jnp.where(meta[2] == 1, -jnp.inf, down[0])
    return jnp.concatenate([above, own[0], below], axis=0)


def y_slots_kernel(slots, meta, up, own, down, table, *refs):
    outs, held = refs[:slots], refs[slots]
    rows = own.shape[1]
    held[...] = y_window(extended(meta, up, own, down), table[...])
    for slot, out in enumerate(outs):
        out[0] = held[slot_rows(meta[0], slot, rows // slots), :]


def y_specs(rows, step):
    specs = [pl.BlockSpec((1, rows, step), lambda z, x, m: (z, 0, x))] * 3
    table = y_table(rows)
    specs.append(pl.BlockSpec(table.shape, lambda z, x, m: (0, 0)))
    return specs, jnp.asarray(table)


def along_y_slots(up, own, down, meta, slots):
    depth, rows, width = own.shape
    step = min(width, 512)
    specs, table = y_specs(rows, step)
    part = rows // slots
    count = own.size
    return pl.pallas_call(
        functools.partial(y_slots_kernel, slots),
        grid_spec=pltpu.PrefetchScalarGridSpec(
            num_scalar_prefetch=1,
            grid=(depth, width // step),
            in_specs=specs,
            out_specs=[pl.BlockSpec((1, part, step), lambda z, x, m: (z, 0, x))] * slots,
            scratch_shapes=[pltpu.VMEM((rows, step), jnp.float32)],
        ),
        out_shape=[jax.ShapeDtypeStruct((depth, part, width), jnp.float32)] * slots,
        compiler_params=params(),
        cost_estimate=cost(3 * 2 * 512 * count, 4 * count, 4 * count),
        name="along_y",
    )(meta, up, own, down, table)


def y_final_kernel(meta, up, own, down, table, outer, *refs):
    dual, density = refs[-2:]
    logs = y_window(extended(meta, up, own, down), table[...])
    dual[0], density[0] = proximal(logs, outer[0])


def along_y_final(up, own, down, external, meta, start, before):
    depth, rows, width = own.shape
    step = min(width, 512)
    specs, table = y_specs(rows, step)
    place = pl.BlockSpec((1, rows, step), lambda z, x, m: (z, 0, x + start // step))
    specs.append(place)
    count = own.size
    shape = jax.ShapeDtypeStruct(external.shape, jnp.float32)
    specs += [pl.BlockSpec(memory_space=pl.ANY)] * len(before)
    return pl.pallas_call(
        y_final_kernel,
        grid_spec=pltpu.PrefetchScalarGridSpec(
            num_scalar_prefetch=1, grid=(depth, width // step), in_specs=specs, out_specs=[place, place]
        ),
        out_shape=[shape, shape],
        input_output_aliases={6 + i: i for i in range(len(before))},
        compiler_params=params(),
        cost_estimate=cost(3 * 2 * 512 * count, 6 * count, 12 * count),
        name="along_y_proximal",
    )(meta, up, own, down, table, external, *before)


def z_kernel(slots, depth, table, *refs):
    ins, outs = refs[:slots], refs[slots:]
    rows, width = ins[0].shape[1:]
    total = slots * depth

    def step(i, carry):
        columns = pl.ds(pl.multiple_of(i * 128, 128), 128)
        values = [ins[k // depth][k % depth, :, columns] for k in range(total)]
        highest_value = jnp.maximum(functools.reduce(jnp.maximum, values), LOWEST)
        weights = [jnp.exp(value - highest_value) for value in values]
        for o in range(total):
            summed = weights[0] * table[o, 0]
            for k in range(1, total):
                summed = summed + weights[k] * table[o, k]
            outs[o // depth][o % depth, :, columns] = jnp.log(summed) + highest_value
        return carry

    lax.fori_loop(0, width // 128, step, 0)


def z_table(place, slots, depth):
    cell = jnp.arange(slots * depth)
    cell = lax.bitwise_xor(cell // depth, place) * depth + cell % depth
    apart = cell[:, None] - cell[None, :]
    distance = apart.astype(jnp.float32)
    values = jnp.exp(-2.0 * distance * distance / float(RADIUS * RADIUS))
    return jnp.where(jnp.abs(apart) <= RADIUS, values, 0.0)


def along_z(parts, table):
    slots = len(parts)
    depth, rows, width = parts[0].shape
    count = slots * parts[0].size
    step = min(width, 512)
    spec = pl.BlockSpec((depth, rows, step), lambda x: (0, 0, x))
    return pl.pallas_call(
        functools.partial(z_kernel, slots, depth),
        grid=(width // step,),
        in_specs=[pl.BlockSpec(memory_space=pltpu.SMEM)] + [spec] * slots,
        out_specs=[spec] * slots,
        out_shape=[jax.ShapeDtypeStruct(parts[0].shape, jnp.float32)] * slots,
        compiler_params=params(),
        cost_estimate=cost(50 * count, 2 * count, 2 * count),
        name="along_z",
    )(table, *parts)


def join_kernel(slots, meta, *refs):
    ins, out = refs[:slots], refs[slots]
    rows = ins[0].shape[1]
    for slot, part in enumerate(ins):
        out[0, slot_rows(meta[0], slot, rows), :] = part[0]


def join(parts, meta):
    slots = len(parts)
    depth, part, width = parts[0].shape
    spec = pl.BlockSpec((1, part, width), lambda z, m: (z, 0, 0))
    shape = (depth, slots * part, width)
    return pl.pallas_call(
        functools.partial(join_kernel, slots),
        grid_spec=pltpu.PrefetchScalarGridSpec(
            num_scalar_prefetch=1,
            grid=(depth,),
            in_specs=[spec] * slots,
            out_specs=pl.BlockSpec((1,) + shape[1:], lambda z, m: (z, 0, 0)),
        ),
        out_shape=jax.ShapeDtypeStruct(shape, jnp.float32),
        compiler_params=params(),
        cost_estimate=cost(0, 2 * depth * slots * part * width, 0),
        name="join",
    )(meta, *parts)


def final_kernel(slots, meta, *refs):
    ins, outer = refs[:slots], refs[slots]
    dual, density = refs[-2:]
    rows = ins[0].shape[1]
    for slot, part in enumerate(ins):
        here = slot_rows(meta[0], slot, rows)
        dual[0, here, :], density[0, here, :] = proximal(part[0], outer[0, here, :])


def final(parts, external, meta, start, before):
    slots = len(parts)
    depth, part, width = parts[0].shape
    step = min(width, 512)
    place = pl.BlockSpec((1, slots * part, step), lambda z, x, m: (z, 0, x + start // step))
    specs = [pl.BlockSpec((1, part, step), lambda z, x, m: (z, 0, x))] * slots + [place]
    specs += [pl.BlockSpec(memory_space=pl.ANY)] * len(before)
    shape = jax.ShapeDtypeStruct(external.shape, jnp.float32)
    count = slots * parts[0].size
    return pl.pallas_call(
        functools.partial(final_kernel, slots),
        grid_spec=pltpu.PrefetchScalarGridSpec(
            num_scalar_prefetch=1, grid=(depth, width // step), in_specs=specs, out_specs=[place, place]
        ),
        out_shape=[shape, shape],
        input_output_aliases={2 + slots + i: i for i in range(len(before))},
        compiler_params=params(),
        cost_estimate=cost(40 * count, 4 * count, 8 * count),
        name="proximal",
    )(meta, *parts, external, *before)


def neighbours(cells):
    ends = lax.axis_size("gy") - 1
    up = lax.ppermute(cells, "gy", [(i, i + 1) for i in range(ends)])
    down = lax.ppermute(cells, "gy", [(i + 1, i) for i in range(ends)])
    return up, down


def exchange(parts):
    count = len(parts)
    order = sorted(range(1, count), key=lambda s: -bin(s).count("1"))
    moved = dict((s, lax.ppermute(parts[s], "gz", [(i, i ^ s) for i in range(count)])) for s in order)
    return [parts[0]] + [moved[s] for s in range(1, count)]


def in_parts(potential, external):
    slots = lax.axis_size("gz")
    depth, rows, length = potential.shape
    half = length // 2
    place, row_place = lax.axis_index("gz"), lax.axis_index("gy")
    meta = jnp.stack(
        [place, (row_place == 0).astype(jnp.int32), (row_place == lax.axis_size("gy") - 1).astype(jnp.int32)]
    ).astype(jnp.int32)
    table = z_table(place, slots, depth)

    parts = along_x(potential, meta, half, half, slots)
    own = along_x(potential, meta, 0, half, 0)
    up, down = neighbours(own)
    parts = exchange(parts)
    parts = along_z(parts, table)
    parts = exchange(parts)
    later = join(parts, meta)
    later_up, later_down = neighbours(later)
    parts = along_y_slots(up, own, down, meta, slots)
    parts = exchange(parts)
    parts = along_z(parts, table)
    parts = exchange(parts)
    outs = along_y_final(later_up, later, later_down, external, meta, half, [])
    return tuple(final(parts, external, meta, 0, outs))


def whole(potential, external):
    depth = RADIUS
    slots = lax.axis_size("gz")
    position, devices = lax.axis_index("gy"), lax.axis_size("gy")
    planes, rows, length = potential.shape

    def table(in_index, out_index):
        apart = in_index[:, None] - out_index[None, :]
        distance = apart.astype(jnp.float32)
        values = jnp.exp(-2.0 * distance * distance / float(RADIUS * RADIUS))
        return jnp.where(jnp.abs(apart) <= RADIUS, values, 0.0)

    def summed(equation, window, axis, kernel):
        highest_value = jnp.max(window, axis=axis, keepdims=True)
        weights = jnp.exp(window - highest_value)
        return jnp.log(jnp.einsum(equation, weights, kernel, precision=HIGHEST)) + highest_value

    border = jnp.full((planes, rows, depth), -jnp.inf, jnp.float32)
    padded = jnp.concatenate([border, potential, border], axis=-1)
    pieces = padded.reshape(planes, rows, length // BLOCK + 1, BLOCK)
    window = jnp.concatenate([pieces[..., :-1, :], pieces[..., 1:, :]], axis=-1)
    kernel = table(jnp.arange(2 * BLOCK) - depth, jnp.arange(BLOCK))
    logs = summed("...w,wo->...o", window, -1, kernel).reshape(potential.shape)

    up, down = neighbours(logs)
    up = jnp.where(position == 0, -jnp.inf, up[:, rows - depth:])
    down = jnp.where(position == devices - 1, -jnp.inf, down[:, :depth])
    window = jnp.concatenate([up, logs, down], axis=1)
    kernel = table(jnp.arange(rows + 2 * depth) - depth, jnp.arange(rows))
    logs = summed("zwx,wo->zox", window, 1, kernel)

    logs = lax.all_to_all(logs, "gz", split_axis=1, concat_axis=0, tiled=True)
    cells = jnp.arange(slots * planes)
    logs = summed("wyx,wo->oyx", logs, 0, table(cells, cells))
    logs = lax.all_to_all(logs, "gz", split_axis=0, concat_axis=1, tiled=True)
    return proximal(logs, external)


def local(potential, external):
    slots = lax.axis_size("gz")
    depth, rows, length = potential.shape
    if slots & (slots - 1) == 0 and rows % (8 * slots) == 0 and slots * depth <= 32 and length % (4 * BLOCK) == 0 and rows == RADIUS:
        return in_parts(potential, external)
    return whole(potential, external)


def solution(mesh):
    return jax.shard_map(
        local,
        mesh=mesh,
        in_specs=(P("gz", "gy", None), P("gz", "gy", None)),
        out_specs=(P("gz", "gy", None), P("gz", "gy", None)),
        check_vma=False,
    )
```

time: 277 us -> 134 us (0.48)
  waiting for transfers between devices: 166 us -> 56 us
  matrix products: 36.1 us -> 0 us
  Pallas kernels: 0 us -> 35.7 us
  local copies, waits for them, and re-layouts: 37.4 us -> 4.93 us
  starting transfers between devices: 26.3 us -> 36.1 us
  other arithmetic: 8.76 us -> 0.17 us
    all_to_all x4 -> x0, waiting for transfers between devices: 111 us -> none  [the longest x1 42.7 us: local(): lax.all_to_all(along_y, 'gz', split_axis=1, concat_axis=0, tiled=True)]
    dot_general x3 -> x0, matrix products: 36.1 us -> none  [the longest x1 13.1 us: along_middle(): summed = jnp.einsum('zwx,wo->zox', weights, kernel_table, precision=HIGHEST)]
    pallas_call x0 -> x8, Pallas kernels: none -> 35.7 us  [the longest x2 10.6 us: along_z(): pl.pallas_call(functools.partial(z_kernel, slots, depth), grid=(width //...]
    ppermute x2 -> x32, starting transfers between devices: 8.6 us -> 36.1 us  [the longest x28 24.1 us: exchange(): lax.ppermute(parts[s], 'gz', [(i, i ^ s) for i in range(count)])]
    all_to_all x4 -> x0, starting transfers between devices: 17.7 us -> none  [the longest x1 4.77 us: local(): lax.all_to_all(along_y, 'gz', split_axis=1, concat_axis=0, tiled=True)]
    all_to_all x4 -> x0, local copies, waits for them, and re-layouts: 9.99 us -> none  [the longest x2 4.22 us: local(): lax.all_to_all(along_y, 'gz', split_axis=1, concat_axis=0, tiled=True)]
    sub x2 -> x0, local copies, waits for them, and re-layouts: 8.88 us -> none  [the longest x1 5.4 us: proximal(): log_level - (log_level + exp_level - shifted) / (1.0 + exp_level)]
    add x2 -> x0, local copies, waits for them, and re-layouts: 6.48 us -> none  [the longest x1 4.11 us: along_middle(): return jnp.log(summed) + highest_value]
  transfers between devices with their start and end apart: 6 -> 32, of which waited for: 5 -> 13; matrix products, arithmetic and copies ran while one was open for 15% -> 0% of each run, Pallas kernels for 0% -> 21%
where the time goes in v1:
time: 134 us
  waiting for transfers between devices  56 us (42%)
  starting transfers between devices  36.1 us (27%)
  Pallas kernels  35.7 us (27%)
  local copies, waits for them, and re-layouts  4.93 us (4%)
    ppermute x28, waiting for transfers between devices, exchange(): lax.ppermute(parts[s], 'gz', [(i, i ^ s) for i in range(count)])  56 us
    ppermute x28, starting transfers between devices, exchange(): lax.ppermute(parts[s], 'gz', [(i, i ^ s) for i in range(count)])  24.1 us
    pallas_call x2, Pallas kernels, along_z(): pl.pallas_call(functools.partial(z_kernel, slots, depth), grid=(width //...  10.6 us
    ppermute x2, starting transfers between devices, neighbours(): up = lax.ppermute(cells, 'gy', [(i, i + 1) for i in range(ends)])  9.29 us
    pallas_call x1, Pallas kernels, along_y_final(): pl.pallas_call(y_final_kernel, grid_spec=pltpu.PrefetchScalarGridSpec(num...  8.07 us
    pallas_call x1, Pallas kernels, along_y_slots(): pl.pallas_call(functools.partial(y_slots_kernel, slots), grid_spec=pltpu....  5.94 us
    pallas_call x2, Pallas kernels, along_x(): pl.pallas_call(functools.partial(x_kernel, first, last, slots, width), gr...  5.78 us
    unnamed x12, local copies, waits for them, and re-layouts  4.93 us
  transfers between devices with their start and end apart: 32, of which 13 were waited for; matrix products, arithmetic and copies ran while one was open for 0% of the time, Pallas kernels for 21%

profile of v1, /device:TPU:0, one launch (start us, length us, event | category | flops | bytes accessed | tf_op | source)
XLA Modules:
  0.0 133.8 jit_solution(9128768216039258364)
XLA Ops:
  0.7 1.9 %copy-done = f32[3,128,2048]{2,1,0:T(8,128)S(1)} copy-done((f32[3,128,2048]{2,1,0:T(8,128)S(1)}, f32[3,128,2048]{2,1,0:T(8,128)}, u32[]{:S(2)}) %copy-start) | copy-done | bytes 3145752
  4.5 2.9 %along_x.3 = (f32[3,16,1024]{2,1,0:T(8,128)S(1)}, f32[3,16,1024]{2,1,0:T(8,128)S(1)}, f32[3,16,1024]{2,1,0:T(8,128)S(1)}, f32[3,16,1024]{2,1,0:T(8,128)S(1)}, f3...) custom-call(s32[3]{0:T(128)S(1)} %pad_add_fusion.meta, ...), custom_call_target="tpu_custom_call" | custom-call | flops 1207959552 | bytes 3145728 | tf_op jit(solution)/shard_map/along_x/pallas_call | solution.py:148
  8.0 2.6 %collective-permute-start.17 = (f32[3,16,1024]{2,1,0:T(8,128)S(1)}, f32[3,16,1024]{2,1,0:T(8,128)S(1)}, u32[]{:S(2)}, u32[]{:S(2)}) collective-permute-start(f32[3,16,1024]{2,1,0:T(8,128)S(1)} %get-tuple-element.54), channel_id=1, source_target_pairs={{0,8},{4,12},{8,0},{12,4},{16,24},{20,28},{24,16},{28,20},{1,9},{5... | collective-permute-start | bytes 589832 | tf_op jit(solution)/shard_map/ppermute | solution.py:346
  10.6 1.8 %collective-permute-start.19 = (f32[3,16,1024]{2,1,0:T(8,128)S(1)}, f32[3,16,1024]{2,1,0:T(8,128)S(1)}, u32[]{:S(2)}, u32[]{:S(2)}) collective-permute-start(f32[3,16,1024]{2,1,0:T(8,128)S(1)} %get-tuple-element.56), channel_id=1, source_target_pairs={{0,16},{4,20},{8,24},{12,28},{16,0},{20,4},{24,8},{28,12},{1,17},{... | collective-permute-start | bytes 589832 | tf_op jit(solution)/shard_map/ppermute | solution.py:346
  12.4 2.8 %along_x.2.own = f32[3,128,1024]{2,1,0:T(8,128)S(1)} custom-call(s32[3]{0:T(128)S(1)} %pad_add_fusion.meta, f32[3,128,2048]{2,1,0:T(8,128)S(1)} %copy-done, f32[3,128,2048]{2,1,0:T(8,128)S(1)} %copy-done, bf16[512,256]{1,0:T(8,128)(2,1)S(1)} %copy-done.3, bf16[512,256]{1,0:T(8,128)(2,1)S(1)} %copy-done.2), custom_call_target="tpu_custom_call" | custom-call | flops 1207959552 | bytes 3145728 | tf_op jit(solution)/shard_map/along_x/pallas_call | solution.py:148
  16.7 4.6 %collective-permute-start = (f32[3,128,1024]{2,1,0:T(8,128)S(1)}, f32[3,128,1024]{2,1,0:T(8,128)S(1)}, u32[]{:S(2)}, u32[]{:S(2)}) collective-permute-start(f32[3,128,1024]{2,1,0:T(8,128)S(1)} %along_x.2.own), channel_id=1, source_target_pairs={{0,1},{1,2},{2,3},{4,5},{5,6},{6,7},{8,9},{9,10},{10,11},{12,13},{... | collective-permute-start | bytes 4718600 | tf_op jit(solution)/shard_map/ppermute | solution.py:338
  21.4 2.0 %collective-permute-start.21 = (f32[3,16,1024]{2,1,0:T(8,128)S(1)}, f32[3,16,1024]{2,1,0:T(8,128)S(1)}, u32[]{:S(2)}, u32[]{:S(2)}) collective-permute-start(f32[3,16,1024]{2,1,0:T(8,128)S(1)} %get-tuple-element.58), channel_id=1, source_target_pairs={{0,24},{4,28},{8,16},{12,20},{16,8},{20,12},{24,0},{28,4},{1,25},{... | collective-permute-start | bytes 589832 | tf_op jit(solution)/shard_map/ppermute | solution.py:346
  24.3 12.5 %collective-permute-done.20.refs_5_ = f32[3,16,1024]{2,1,0:T(8,128)S(1)} collective-permute-done((f32[3,16,1024]{2,1,0:T(8,128)S(1)}, f32[3,16,1024]{2,1,0:T(8,128)S(1)}, u32[]{:S(2)}, u32[]{:S(2)}) %collective-permute-start.20) | collective-permute-done | bytes 196640 | tf_op jit(solution)/shard_map/ppermute | solution.py:346
  36.7 5.3 %along_z.3 = (f32[3,16,1024]{2,1,0:T(8,128)S(1)}, f32[3,16,1024]{2,1,0:T(8,128)S(1)}, f32[3,16,1024]{2,1,0:T(8,128)S(1)}, f32[3,16,1024]{2,1,0:T(8,128)S(1)}, f3...) custom-call(f32[24,24]{1,0:T(8,128)S(1)} %fusion.3.table, ...), custom_call_target="tpu_custom_call" | custom-call | flops 19660800 | bytes 3145728 | tf_op jit(solution)/shard_map/along_z/pallas_call | solution.py:266
  44.5 5.3 %collective-permute-done.24.refs_2_ = f32[3,16,1024]{2,1,0:T(8,128)S(1)} collective-permute-done((f32[3,16,1024]{2,1,0:T(8,128)S(1)}, f32[3,16,1024]{2,1,0:T(8,128)S(1)}, u32[]{:S(2)}, u32[]{:S(2)}) %collective-permute-start.24) | collective-permute-done | bytes 196640 | tf_op jit(solution)/shard_map/ppermute | solution.py:346
  49.9 3.3 %collective-permute-done.25.refs_3_ = f32[3,16,1024]{2,1,0:T(8,128)S(1)} collective-permute-done((f32[3,16,1024]{2,1,0:T(8,128)S(1)}, f32[3,16,1024]{2,1,0:T(8,128)S(1)}, u32[]{:S(2)}, u32[]{:S(2)}) %collective-permute-start.25) | collective-permute-done | bytes 196640 | tf_op jit(solution)/shard_map/ppermute | solution.py:346
  56.5 5.3 %collective-permute-done.28.refs_6_ = f32[3,16,1024]{2,1,0:T(8,128)S(1)} collective-permute-done((f32[3,16,1024]{2,1,0:T(8,128)S(1)}, f32[3,16,1024]{2,1,0:T(8,128)S(1)}, u32[]{:S(2)}, u32[]{:S(2)}) %collective-permute-start.28) | collective-permute-done | bytes 196640 | tf_op jit(solution)/shard_map/ppermute | solution.py:346
  61.8 3.6 %collective-permute-done.29.refs_7_ = f32[3,16,1024]{2,1,0:T(8,128)S(1)} collective-permute-done((f32[3,16,1024]{2,1,0:T(8,128)S(1)}, f32[3,16,1024]{2,1,0:T(8,128)S(1)}, u32[]{:S(2)}, u32[]{:S(2)}) %collective-permute-start.29) | collective-permute-done | bytes 196640 | tf_op jit(solution)/shard_map/ppermute | solution.py:346
  67.4 4.6 %collective-permute-start.30 = (f32[3,128,1024]{2,1,0:T(8,128)S(1)}, f32[3,128,1024]{2,1,0:T(8,128)S(1)}, u32[]{:S(2)}, u32[]{:S(2)}) collective-permute-start(f32[3,128,1024]{2,1,0:T(8,128)S(1)} %join.1.own), channel_id=1, source_target_pairs={{0,1},{1,2},{2,3},{4,5},{5,6},{6,7},{8,9},{9,10},{10,11},{12,13},{... | collective-permute-start | bytes 4718600 | tf_op jit(solution)/shard_map/ppermute | solution.py:338
  73.2 5.9 %along_y.1 = (f32[3,16,1024]{2,1,0:T(8,128)S(1)}, f32[3,16,1024]{2,1,0:T(8,128)S(1)}, f32[3,16,1024]{2,1,0:T(8,128)S(1)}, f32[3,16,1024]{2,1,0:T(8,128)S(1)}, f3...) custom-call(s32[3]{0:T(128)S(1)} %pad_add_fusion.meta, ...), custom_call_target="tpu_custom_call" | custom-call | flops 1207959552 | bytes 6291456 | tf_op jit(solution)/shard_map/along_y/pallas_call | solution.py:187
  81.7 5.3 %collective-permute-done.3.refs_2_ = f32[3,16,1024]{2,1,0:T(8,128)S(1)} collective-permute-done((f32[3,16,1024]{2,1,0:T(8,128)S(1)}, f32[3,16,1024]{2,1,0:T(8,128)S(1)}, u32[]{:S(2)}, u32[]{:S(2)}) %collective-permute-start.3) | collective-permute-done | bytes 196640 | tf_op jit(solution)/shard_map/ppermute | solution.py:346
  87.0 3.3 %collective-permute-done.4.refs_3_ = f32[3,16,1024]{2,1,0:T(8,128)S(1)} collective-permute-done((f32[3,16,1024]{2,1,0:T(8,128)S(1)}, f32[3,16,1024]{2,1,0:T(8,128)S(1)}, u32[]{:S(2)}, u32[]{:S(2)}) %collective-permute-start.4) | collective-permute-done | bytes 196640 | tf_op jit(solution)/shard_map/ppermute | solution.py:346
  93.6 5.3 %collective-permute-done.7.refs_6_ = f32[3,16,1024]{2,1,0:T(8,128)S(1)} collective-permute-done((f32[3,16,1024]{2,1,0:T(8,128)S(1)}, f32[3,16,1024]{2,1,0:T(8,128)S(1)}, u32[]{:S(2)}, u32[]{:S(2)}) %collective-permute-start.7) | collective-permute-done | bytes 196640 | tf_op jit(solution)/shard_map/ppermute | solution.py:346
  98.9 3.6 %collective-permute-done.8.refs_7_ = f32[3,16,1024]{2,1,0:T(8,128)S(1)} collective-permute-done((f32[3,16,1024]{2,1,0:T(8,128)S(1)}, f32[3,16,1024]{2,1,0:T(8,128)S(1)}, u32[]{:S(2)}, u32[]{:S(2)}) %collective-permute-start.8) | collective-permute-done | bytes 196640 | tf_op jit(solution)/shard_map/ppermute | solution.py:346
  102.5 5.3 %along_z.2 = (f32[3,16,1024]{2,1,0:T(8,128)S(1)}, f32[3,16,1024]{2,1,0:T(8,128)S(1)}, f32[3,16,1024]{2,1,0:T(8,128)S(1)}, f32[3,16,1024]{2,1,0:T(8,128)S(1)}, f3...) custom-call(f32[24,24]{1,0:T(8,128)S(1)} %fusion.3.table, ...), custom_call_target="tpu_custom_call" | custom-call | flops 19660800 | bytes 3145728 | tf_op jit(solution)/shard_map/along_z/pallas_call | solution.py:266
  113.3 2.5 %collective-permute-done.10.refs_2_ = f32[3,16,1024]{2,1,0:T(8,128)S(1)} collective-permute-done((f32[3,16,1024]{2,1,0:T(8,128)S(1)}, f32[3,16,1024]{2,1,0:T(8,128)S(1)}, u32[]{:S(2)}, u32[]{:S(2)}) %collective-permute-start.10) | collective-permute-done | bytes 196640 | tf_op jit(solution)/shard_map/ppermute | solution.py:346
  116.1 8.1 %along_y_proximal.1 = (f32[3,128,2048]{2,1,0:T(8,128)}, f32[3,128,2048]{2,1,0:T(8,128)}) custom-call(s32[3]{0:T(128)S(1)} %pad_add_fusion.meta, f32[3,128,1024]{2,1,0:T(8,128)S(1)} %collective-permute-done.30.up, f32[3,128,1024]{2,1,0:T(8,128)S(1)} %join.1.own, f32[3,128,1024]{2,1,0:T(8,128)S(1)} %collective-permute-done.31.down, ...), custom_call_target="tpu_custom_call" | custom-call | flops 1207959552 | bytes 9437184 | tf_op jit(solution)/shard_map/along_y_proximal/pallas_call | solution.py:218
  124.2 5.0 %collective-permute-done.13.refs_5_ = f32[3,16,1024]{2,1,0:T(8,128)S(1)} collective-permute-done((f32[3,16,1024]{2,1,0:T(8,128)S(1)}, f32[3,16,1024]{2,1,0:T(8,128)S(1)}, u32[]{:S(2)}, u32[]{:S(2)}) %collective-permute-start.13) | collective-permute-done | bytes 196640 | tf_op jit(solution)/shard_map/ppermute | solution.py:346
  129.2 4.6 %proximal.1 = (f32[3,128,2048]{2,1,0:T(8,128)}, f32[3,128,2048]{2,1,0:T(8,128)}) custom-call(s32[3]{0:T(128)S(1)} %pad_add_fusion.meta, f32[3,16,1024]{2,1,0:T(8,128)S(1)} %get-tuple-element.44.refs_0_, f32[3,16,1024]{2,1,0:T(8,128)S(1)} %collective-permute-done.9.refs_1_, ...), custom_call_target="tpu_custom_call", output_to_operand_aliasing={{0}: (10, {}), {1}: (11, {})} | custom-call | flops 15728640 | bytes 6291456 | tf_op jit(solution)/shard_map/proximal/pallas_call | solution.py:323
  (63 shorter events, 25.4 us)
Async XLA Ops:
  7.5 9.2 %collective-permute-start.16 = (f32[3,16,1024]{2,1,0:T(8,128)S(1)}, f32[3,16,1024]{2,1,0:T(8,128)S(1)}, u32[]{:S(2)}, u32[]{:S(2)}) collective-permute-start(f32[3,16,1024]{2,1,0:T(8,128)S(1)} %get-tuple-element.53), channel_id=1, source_target_pairs={{0,4},{4,0},{8,12},{12,8},{16,20},{20,16},{24,28},{28,24},{1,5},{5... | collective-permute-start | bytes 589832 | tf_op jit(solution)/shard_map/ppermute | solution.py:346
  8.0 13.4 %collective-permute-start.17 = (f32[3,16,1024]{2,1,0:T(8,128)S(1)}, f32[3,16,1024]{2,1,0:T(8,128)S(1)}, u32[]{:S(2)}, u32[]{:S(2)}) collective-permute-start(f32[3,16,1024]{2,1,0:T(8,128)S(1)} %get-tuple-element.54), channel_id=1, source_target_pairs={{0,8},{4,12},{8,0},{12,4},{16,24},{20,28},{24,16},{28,20},{1,9},{5... | collective-permute-start | bytes 589832 | tf_op jit(solution)/shard_map/ppermute | solution.py:346
  10.5 10.9 %collective-permute-start.18 = (f32[3,16,1024]{2,1,0:T(8,128)S(1)}, f32[3,16,1024]{2,1,0:T(8,128)S(1)}, u32[]{:S(2)}, u32[]{:S(2)}) collective-permute-start(f32[3,16,1024]{2,1,0:T(8,128)S(1)} %get-tuple-element.55), channel_id=1, source_target_pairs={{0,12},{4,8},{8,4},{12,0},{16,28},{20,24},{24,20},{28,16},{1,13},{... | collective-permute-start | bytes 589832 | tf_op jit(solution)/shard_map/ppermute | solution.py:346
  10.6 12.9 %collective-permute-start.19 = (f32[3,16,1024]{2,1,0:T(8,128)S(1)}, f32[3,16,1024]{2,1,0:T(8,128)S(1)}, u32[]{:S(2)}, u32[]{:S(2)}) collective-permute-start(f32[3,16,1024]{2,1,0:T(8,128)S(1)} %get-tuple-element.56), channel_id=1, source_target_pairs={{0,16},{4,20},{8,24},{12,28},{16,0},{20,4},{24,8},{28,12},{1,17},{... | collective-permute-start | bytes 589832 | tf_op jit(solution)/shard_map/ppermute | solution.py:346
  15.2 56.9 %collective-permute-start.1 = (f32[3,128,1024]{2,1,0:T(8,128)S(1)}, f32[3,128,1024]{2,1,0:T(8,128)S(1)}, u32[]{:S(2)}, u32[]{:S(2)}) collective-permute-start(f32[3,128,1024]{2,1,0:T(8,128)S(1)} %along_x.2.own), channel_id=1, source_target_pairs={{1,0},{2,1},{3,2},{5,4},{6,5},{7,6},{9,8},{10,9},{11,10},{13,12},{... | collective-permute-start | bytes 4718600 | tf_op jit(solution)/shard_map/ppermute | solution.py:339
  16.7 55.4 %collective-permute-start = (f32[3,128,1024]{2,1,0:T(8,128)S(1)}, f32[3,128,1024]{2,1,0:T(8,128)S(1)}, u32[]{:S(2)}, u32[]{:S(2)}) collective-permute-start(f32[3,128,1024]{2,1,0:T(8,128)S(1)} %along_x.2.own), channel_id=1, source_target_pairs={{0,1},{1,2},{2,3},{4,5},{5,6},{6,7},{8,9},{9,10},{10,11},{12,13},{... | collective-permute-start | bytes 4718600 | tf_op jit(solution)/shard_map/ppermute | solution.py:338
  21.4 15.4 %collective-permute-start.20 = (f32[3,16,1024]{2,1,0:T(8,128)S(1)}, f32[3,16,1024]{2,1,0:T(8,128)S(1)}, u32[]{:S(2)}, u32[]{:S(2)}) collective-permute-start(f32[3,16,1024]{2,1,0:T(8,128)S(1)} %get-tuple-element.57), channel_id=1, source_target_pairs={{0,20},{4,16},{8,28},{12,24},{16,4},{20,0},{24,12},{28,8},{1,21},{... | collective-permute-start | bytes 589832 | tf_op jit(solution)/shard_map/ppermute | solution.py:346
  21.4 15.3 %collective-permute-start.21 = (f32[3,16,1024]{2,1,0:T(8,128)S(1)}, f32[3,16,1024]{2,1,0:T(8,128)S(1)}, u32[]{:S(2)}, u32[]{:S(2)}) collective-permute-start(f32[3,16,1024]{2,1,0:T(8,128)S(1)} %get-tuple-element.58), channel_id=1, source_target_pairs={{0,24},{4,28},{8,16},{12,20},{16,8},{20,12},{24,0},{28,4},{1,25},{... | collective-permute-start | bytes 589832 | tf_op jit(solution)/shard_map/ppermute | solution.py:346
  23.5 13.2 %collective-permute-start.22 = (f32[3,16,1024]{2,1,0:T(8,128)S(1)}, f32[3,16,1024]{2,1,0:T(8,128)S(1)}, u32[]{:S(2)}, u32[]{:S(2)}) collective-permute-start(f32[3,16,1024]{2,1,0:T(8,128)S(1)} %get-tuple-element.59), channel_id=1, source_target_pairs={{0,28},{4,24},{8,20},{12,16},{16,12},{20,8},{24,4},{28,0},{1,29},{... | collective-permute-start | bytes 589832 | tf_op jit(solution)/shard_map/ppermute | solution.py:346
  43.7 9.5 %collective-permute-start.25 = (f32[3,16,1024]{2,1,0:T(8,128)S(1)}, f32[3,16,1024]{2,1,0:T(8,128)S(1)}, u32[]{:S(2)}, u32[]{:S(2)}) collective-permute-start(f32[3,16,1024]{2,1,0:T(8,128)S(1)} %get-tuple-element.63), channel_id=1, source_target_pairs={{0,12},{4,8},{8,4},{12,0},{16,28},{20,24},{24,20},{28,16},{1,13},{... | collective-permute-start | bytes 589832 | tf_op jit(solution)/shard_map/ppermute | solution.py:346
  44.0 10.7 %collective-permute-start.26 = (f32[3,16,1024]{2,1,0:T(8,128)S(1)}, f32[3,16,1024]{2,1,0:T(8,128)S(1)}, u32[]{:S(2)}, u32[]{:S(2)}) collective-permute-start(f32[3,16,1024]{2,1,0:T(8,128)S(1)} %get-tuple-element.64), channel_id=1, source_target_pairs={{0,16},{4,20},{8,24},{12,28},{16,0},{20,4},{24,8},{28,12},{1,17},{... | collective-permute-start | bytes 589832 | tf_op jit(solution)/shard_map/ppermute | solution.py:346
  53.2 8.6 %collective-permute-start.28 = (f32[3,16,1024]{2,1,0:T(8,128)S(1)}, f32[3,16,1024]{2,1,0:T(8,128)S(1)}, u32[]{:S(2)}, u32[]{:S(2)}) collective-permute-start(f32[3,16,1024]{2,1,0:T(8,128)S(1)} %get-tuple-element.66), channel_id=1, source_target_pairs={{0,24},{4,28},{8,16},{12,20},{16,8},{20,12},{24,0},{28,4},{1,25},{... | collective-permute-start | bytes 589832 | tf_op jit(solution)/shard_map/ppermute | solution.py:346
  54.7 10.7 %collective-permute-start.29 = (f32[3,16,1024]{2,1,0:T(8,128)S(1)}, f32[3,16,1024]{2,1,0:T(8,128)S(1)}, u32[]{:S(2)}, u32[]{:S(2)}) collective-permute-start(f32[3,16,1024]{2,1,0:T(8,128)S(1)} %get-tuple-element.67), channel_id=1, source_target_pairs={{0,28},{4,24},{8,20},{12,16},{16,12},{20,8},{24,4},{28,0},{1,29},{... | collective-permute-start | bytes 589832 | tf_op jit(solution)/shard_map/ppermute | solution.py:346
  66.1 43.6 %collective-permute-start.31 = (f32[3,128,1024]{2,1,0:T(8,128)S(1)}, f32[3,128,1024]{2,1,0:T(8,128)S(1)}, u32[]{:S(2)}, u32[]{:S(2)}) collective-permute-start(f32[3,128,1024]{2,1,0:T(8,128)S(1)} %join.1.own), channel_id=1, source_target_pairs={{1,0},{2,1},{3,2},{5,4},{6,5},{7,6},{9,8},{10,9},{11,10},{13,12},{... | collective-permute-start | bytes 4718600 | tf_op jit(solution)/shard_map/ppermute | solution.py:339
  67.4 43.0 %collective-permute-start.30 = (f32[3,128,1024]{2,1,0:T(8,128)S(1)}, f32[3,128,1024]{2,1,0:T(8,128)S(1)}, u32[]{:S(2)}, u32[]{:S(2)}) collective-permute-start(f32[3,128,1024]{2,1,0:T(8,128)S(1)} %join.1.own), channel_id=1, source_target_pairs={{0,1},{1,2},{2,3},{4,5},{5,6},{6,7},{8,9},{9,10},{10,11},{12,13},{... | collective-permute-start | bytes 4718600 | tf_op jit(solution)/shard_map/ppermute | solution.py:338
  80.8 9.5 %collective-permute-start.4 = (f32[3,16,1024]{2,1,0:T(8,128)S(1)}, f32[3,16,1024]{2,1,0:T(8,128)S(1)}, u32[]{:S(2)}, u32[]{:S(2)}) collective-permute-start(f32[3,16,1024]{2,1,0:T(8,128)S(1)} %get-tuple-element.39), channel_id=1, source_target_pairs={{0,12},{4,8},{8,4},{12,0},{16,28},{20,24},{24,20},{28,16},{1,13},{... | collective-permute-start | bytes 589832 | tf_op jit(solution)/shard_map/ppermute | solution.py:346
  81.1 10.9 %collective-permute-start.5 = (f32[3,16,1024]{2,1,0:T(8,128)S(1)}, f32[3,16,1024]{2,1,0:T(8,128)S(1)}, u32[]{:S(2)}, u32[]{:S(2)}) collective-permute-start(f32[3,16,1024]{2,1,0:T(8,128)S(1)} %get-tuple-element.40), channel_id=1, source_target_pairs={{0,16},{4,20},{8,24},{12,28},{16,0},{20,4},{24,8},{28,12},{1,17},{... | collective-permute-start | bytes 589832 | tf_op jit(solution)/shard_map/ppermute | solution.py:346
  90.3 8.6 %collective-permute-start.7 = (f32[3,16,1024]{2,1,0:T(8,128)S(1)}, f32[3,16,1024]{2,1,0:T(8,128)S(1)}, u32[]{:S(2)}, u32[]{:S(2)}) collective-permute-start(f32[3,16,1024]{2,1,0:T(8,128)S(1)} %get-tuple-element.42), channel_id=1, source_target_pairs={{0,24},{4,28},{8,16},{12,20},{16,8},{20,12},{24,0},{28,4},{1,25},{... | collective-permute-start | bytes 589832 | tf_op jit(solution)/shard_map/ppermute | solution.py:346
  92.1 10.4 %collective-permute-start.8 = (f32[3,16,1024]{2,1,0:T(8,128)S(1)}, f32[3,16,1024]{2,1,0:T(8,128)S(1)}, u32[]{:S(2)}, u32[]{:S(2)}) collective-permute-start(f32[3,16,1024]{2,1,0:T(8,128)S(1)} %get-tuple-element.43), channel_id=1, source_target_pairs={{0,28},{4,24},{8,20},{12,16},{16,12},{20,8},{24,4},{28,0},{1,29},{... | collective-permute-start | bytes 589832 | tf_op jit(solution)/shard_map/ppermute | solution.py:346
  109.5 14.6 %collective-permute-start.11 = (f32[3,16,1024]{2,1,0:T(8,128)S(1)}, f32[3,16,1024]{2,1,0:T(8,128)S(1)}, u32[]{:S(2)}, u32[]{:S(2)}) collective-permute-start(f32[3,16,1024]{2,1,0:T(8,128)S(1)} %get-tuple-element.47), channel_id=1, source_target_pairs={{0,12},{4,8},{8,4},{12,0},{16,28},{20,24},{24,20},{28,16},{1,13},{... | collective-permute-start | bytes 589832 | tf_op jit(solution)/shard_map/ppermute | solution.py:346
  109.8 14.4 %collective-permute-start.12 = (f32[3,16,1024]{2,1,0:T(8,128)S(1)}, f32[3,16,1024]{2,1,0:T(8,128)S(1)}, u32[]{:S(2)}, u32[]{:S(2)}) collective-permute-start(f32[3,16,1024]{2,1,0:T(8,128)S(1)} %get-tuple-element.48), channel_id=1, source_target_pairs={{0,16},{4,20},{8,24},{12,28},{16,0},{20,4},{24,8},{28,12},{1,17},{... | collective-permute-start | bytes 589832 | tf_op jit(solution)/shard_map/ppermute | solution.py:346
  110.4 18.8 %collective-permute-start.13 = (f32[3,16,1024]{2,1,0:T(8,128)S(1)}, f32[3,16,1024]{2,1,0:T(8,128)S(1)}, u32[]{:S(2)}, u32[]{:S(2)}) collective-permute-start(f32[3,16,1024]{2,1,0:T(8,128)S(1)} %get-tuple-element.49), channel_id=1, source_target_pairs={{0,20},{4,16},{8,28},{12,24},{16,4},{20,0},{24,12},{28,8},{1,21},{... | collective-permute-start | bytes 589832 | tf_op jit(solution)/shard_map/ppermute | solution.py:346
  111.6 17.6 %collective-permute-start.14 = (f32[3,16,1024]{2,1,0:T(8,128)S(1)}, f32[3,16,1024]{2,1,0:T(8,128)S(1)}, u32[]{:S(2)}, u32[]{:S(2)}) collective-permute-start(f32[3,16,1024]{2,1,0:T(8,128)S(1)} %get-tuple-element.50), channel_id=1, source_target_pairs={{0,24},{4,28},{8,16},{12,20},{16,8},{20,12},{24,0},{28,4},{1,25},{... | collective-permute-start | bytes 589832 | tf_op jit(solution)/shard_map/ppermute | solution.py:346
  115.8 13.4 %collective-permute-start.15 = (f32[3,16,1024]{2,1,0:T(8,128)S(1)}, f32[3,16,1024]{2,1,0:T(8,128)S(1)}, u32[]{:S(2)}, u32[]{:S(2)}) collective-permute-start(f32[3,16,1024]{2,1,0:T(8,128)S(1)} %get-tuple-element.51), channel_id=1, source_target_pairs={{0,28},{4,24},{8,20},{12,16},{16,12},{20,8},{24,4},{28,0},{1,29},{... | collective-permute-start | bytes 589832 | tf_op jit(solution)/shard_map/ppermute | solution.py:346
  (14 other events, 120.5 us)

commit v2 on v0

v2 whole, which is shorter than its diff:
```python
import functools

import jax
import jax.numpy as jnp
import ml_dtypes
import numpy as np
from jax import lax
from jax.experimental import pallas as pl
from jax.experimental.pallas import tpu as pltpu
from jax.sharding import PartitionSpec as P

RADIUS = 128
BLOCK = 2 * RADIUS
VMEM_BYTES = 24 * 1024 * 1024
LOWEST = -1e30

HIGHEST = lax.Precision.HIGHEST


def gauss(apart):
    apart = np.asarray(apart, np.float64)
    table = np.exp(-2.0 * apart * apart / float(RADIUS * RADIUS))
    return np.where(np.abs(apart) <= RADIUS, table, 0.0)


def two_terms(table):
    high = table.astype(ml_dtypes.bfloat16)
    low = (table - high.astype(np.float64)).astype(ml_dtypes.bfloat16)
    return high, low


def x_tables():
    table = gauss(np.arange(2 * BLOCK)[:, None] - RADIUS - np.arange(BLOCK)[None, :])
    return two_terms(table)


def y_table(rows):
    table = gauss(np.arange(rows + 2 * RADIUS)[None, :] - RADIUS - np.arange(rows)[:, None])
    before, own, behind = np.split(table, [RADIUS, RADIUS + rows], axis=1)
    tables = [[behind, own, before], [before, own, behind]]
    return np.concatenate([term for blocks in tables for term in two_terms(np.concatenate(blocks, axis=1))], axis=0)


def split(weights):
    high = weights.astype(jnp.bfloat16)
    low = (weights - high.astype(jnp.float32)).astype(jnp.bfloat16)
    return high, low


def dot(a, b):
    return jnp.dot(a, b, preferred_element_type=jnp.float32)


def x_window(window, high_table, low_table):
    highest_value = jnp.max(window, axis=-1, keepdims=True)
    high, low = split(jnp.exp(window - highest_value))
    summed = dot(high, high_table) + (dot(low, high_table) + dot(high, low_table))
    return jnp.log(summed) + highest_value


def two_term_sum(table, weights):
    rows = table.shape[0] // 2
    high, low = split(weights)
    both = dot(table, high)
    return both[:rows] + (both[rows:] + dot(table[:rows], low))


def y_window(window, table):
    highest_value = jnp.max(window, axis=0, keepdims=True)
    return jnp.log(two_term_sum(table, jnp.exp(window - highest_value))) + highest_value


def proximal(logs, outer_field):
    shifted = logs - 0.5 * outer_field
    level = 1.0 + (jnp.maximum(shifted, 0.0) + jnp.log(1.0 + jnp.exp(-jnp.abs(shifted))))
    log_level = jnp.log(level)
    for newton_step in range(2):
        if newton_step:
            level = jnp.exp(log_level)
        log_level = (level * (log_level - 1.0) + shifted) / (1.0 + level)
    return log_level - logs, log_level


def slot_rows(place, slot, rows):
    return pl.ds(pl.multiple_of(lax.bitwise_xor(place, slot) * rows, rows), rows)


def all_of(array):
    return pl.BlockSpec(array.shape, lambda i, m: (0,) * array.ndim)


def call(kernel, name, meta, operands, outs, work, aliases={}, scratch=(), after=(), after_far=False, in_place=False):
    used = 1 + len(operands)
    if after_far:
        after = [pltpu.with_memory_space_constraint(array, pltpu.HBM) for array in after]
    operands = operands + [(array, pl.BlockSpec(memory_space=pl.ANY)) for array in after]

    def body(*refs):
        kernel(*refs[:used], *refs[used + len(after) :])

    shapes = [jax.ShapeDtypeStruct(shape, jnp.float32) for shape in outs]
    return pl.pallas_call(
        body,
        grid_spec=pltpu.PrefetchScalarGridSpec(
            num_scalar_prefetch=1,
            grid=(1,),
            in_specs=[spec for _, spec in operands],
            out_specs=[pl.BlockSpec(memory_space=pltpu.HBM) if in_place else all_of(shape) for shape in shapes],
            scratch_shapes=list(scratch),
        ),
        out_shape=shapes,
        input_output_aliases=aliases,
        compiler_params=pltpu.CompilerParams(vmem_limit_bytes=VMEM_BYTES),
        cost_estimate=pl.CostEstimate(
            flops=2 * work[0], bytes_accessed=8 * sum(int(np.prod(shape)) for shape in outs), transcendentals=work[1]
        ),
        name=name,
    )(meta, *[array for array, _ in operands])


def x_kernel(edges, received, parts, meta, main, left, right, high_ref, low_ref, *refs):
    refs = list(refs)
    other = refs.pop(0) if received else None
    held = refs.pop() if parts else None
    depth, rows, width = main.shape
    own = slice(0, depth)

    def ended(edge, which):
        return jnp.where(meta[3] == which - 1, -jnp.inf, edge) if which else edge

    cells = [ended(left[...], edges[0]), main[...], ended(right[...], edges[1])]
    cells = jnp.concatenate([piece.reshape(depth * rows, piece.shape[-1]) for piece in cells], axis=-1)
    for j in range(width // BLOCK):
        window = cells[:, j * BLOCK : (j + 2) * BLOCK]
        result = x_window(window, high_ref[...], low_ref[...]).reshape(depth, rows, BLOCK)
        columns = pl.ds(j * BLOCK, BLOCK)
        if parts:
            held[:, :, columns] = result
        else:
            refs[0][own, :, columns] = result
    if parts:
        for slot, out in enumerate(refs):
            here = slot_rows(meta[0], slot, rows // parts)
            out[own] = held[:, here, :]
            out[depth:] = other[:, here, :]
    elif received:
        refs[0][depth:] = other[...]


def along_x(potential, meta, mine, start, width, parts, received=None, after=(), far=False):
    depth, rows, length = potential.shape
    half = length // 2

    def begin(m, unit):
        return (m[3] if mine else 1 - m[3]) * (half // unit) + start // unit

    edges = (0 if start else (1 if mine else 2)), (0 if start + width < half else (2 if mine else 1))
    before = lambda i, m: (0, 0, jnp.maximum(begin(m, RADIUS) - 1, 0))
    behind = lambda i, m: (0, 0, jnp.minimum(begin(m, RADIUS) + width // RADIUS, length // RADIUS - 1))
    operands = [
        (potential, pl.BlockSpec((depth, rows, width), lambda i, m: (0, 0, begin(m, width)))),
        (potential, pl.BlockSpec((depth, rows, RADIUS), before)),
        (potential, pl.BlockSpec((depth, rows, RADIUS), behind)),
    ]
    operands += [(jnp.asarray(table), all_of(table)) for table in x_tables()]
    if far:
        operands = [(pltpu.with_memory_space_constraint(array, pltpu.HBM), spec) for array, spec in operands]
    planes = depth
    if received is not None:
        planes = 2 * depth
        operands.append((received, all_of(received)))
    outs = [(planes, rows // parts, width)] * parts if parts else [(planes, rows, width)]
    count = depth * rows * width
    return call(
        functools.partial(x_kernel, edges, received is not None, parts),
        "along_x", meta, operands, outs, (6 * BLOCK * count, 3 * count),
        scratch=[pltpu.VMEM((depth, rows, width), jnp.float32)] if parts else [], after=after,
    )


def along_y(meta, cells, plane, table):
    paired, own, other = cells
    cells = [
        jnp.where(meta[1] == 1, -jnp.inf, paired[plane]),
        own[plane],
        jnp.where(meta[2] == 1, -jnp.inf, other[plane]),
    ]
    return y_window(jnp.concatenate(cells, axis=0), table[...])


def y_operands(cells, planes, first=0):
    rows, width = cells[1].shape[1:]
    operands = [(array, pl.BlockSpec((planes, rows, width), lambda i, m: (first // planes, 0, 0))) for array in cells]
    table = y_table(rows)
    return operands + [(jnp.asarray(table), pl.BlockSpec((2 * rows, table.shape[1]), lambda i, m: (m[4], 0)))]


def y_work(count):
    return 12 * RADIUS * count, 4 * count


def y_parts_kernel(meta, paired, own, other, table, *refs):
    outs, held = refs[:-1], refs[-1]
    planes, rows, width = own.shape
    for plane in range(planes):
        held[plane] = along_y(meta, (paired, own, other), plane, table)
    for slot, out in enumerate(outs):
        out[...] = held[:, slot_rows(meta[0], slot, rows // len(outs)), :]


def along_y_parts(cells, meta, parts, after=()):
    planes, rows, width = cells[1].shape
    return call(
        y_parts_kernel, "along_y", meta, y_operands(cells, planes), [(planes, rows // parts, width)] * parts,
        y_work(cells[1].size), scratch=[pltpu.VMEM((planes, rows, width), jnp.float32)], after=after,
    )


def y_send_kernel(meta, paired, own, other, table, out):
    for plane in range(out.shape[0]):
        out[plane] = along_y(meta, (paired, own, other), plane, table)


def along_y_send(cells, meta, first, after=()):
    planes, rows, width = cells[1].shape
    planes -= first
    return call(
        y_send_kernel, "along_y", meta, y_operands(cells, planes, first), [(planes, rows, width)], y_work(cells[1].size // 2),
        after=after,
    )[0]


def z_kernel(meta, table, *refs):
    count = len(refs) // 2
    ins, outs = refs[:count], refs[count:]
    planes, rows, width = ins[0].shape
    kernel = table[...]
    for tile in range(rows // 8):
        here = pl.ds(8 * tile, 8)
        for begin in range(0, width, BLOCK):
            columns = pl.ds(begin, min(BLOCK, width - begin))
            values = [part[k, here, columns] for part in ins for k in range(planes)]
            highest_value = jnp.maximum(functools.reduce(jnp.maximum, values), LOWEST)
            weights = jnp.concatenate([jnp.exp(value - highest_value) for value in values], axis=0)
            logs = jnp.log(two_term_sum(kernel, weights))
            for o in range(count * planes):
                outs[o // planes][o % planes, here, columns] = logs[8 * o : 8 * o + 8] + highest_value


def z_table(place, slots, depth):
    cell = jnp.arange(slots * depth * 8) // 8
    row = jnp.arange(slots * depth * 8) % 8
    cell = lax.bitwise_xor(cell // depth, place) * depth + cell % depth
    apart = cell[:, None] - cell[None, :]
    distance = apart.astype(jnp.float32)
    values = jnp.exp(-2.0 * distance * distance / float(RADIUS * RADIUS))
    values = jnp.where((jnp.abs(apart) <= RADIUS) & (row[:, None] == row[None, :]), values, 0.0)
    high = lax.reduce_precision(values, 8, 7)
    return jnp.concatenate([high, values - high], axis=0).astype(jnp.bfloat16)


def along_z(parts, table, meta):
    count = len(parts) * parts[0].size
    return call(
        z_kernel, "along_z", meta, [(array, all_of(array)) for array in [table] + parts], [part.shape for part in parts],
        (768 * count, 2 * count),
    )


def join_kernel(meta, *refs):
    ins, out = refs[:-1], refs[-1]
    for slot, part in enumerate(ins):
        out[:, slot_rows(meta[0], slot, part.shape[1]), :] = part[...]


def join(parts, meta, first=0, after=(), after_far=False):
    planes, part, width = parts[0].shape
    block = planes - first
    spec = pl.BlockSpec((block, part, width), lambda i, m: (first // block, 0, 0))
    return call(
        join_kernel, "join", meta, [(array, spec) for array in parts], [(block, part * len(parts), width)], (0, 0), after=after,
        after_far=after_far,
    )[0]


def final_kernel(pieces, meta, *refs):
    refs = list(refs)
    ins = [[refs.pop(0) for _ in range(count + 1)] for count, _, _ in pieces]
    results, sems = refs[-1 - len(pieces) : -1], refs[-1]
    outs = refs[-3 - len(pieces) : -1 - len(pieces)]
    depth = ins[0][-1].shape[0]
    half = outs[0].shape[2] // 2
    copies = []
    for at, (count, mine, start) in enumerate(pieces):
        cells, outer, held = ins[at][:-1], ins[at][-1], results[at]
        width = outer.shape[2]
        column = pl.multiple_of((meta[3] if mine else 1 - meta[3]) * half + start, width)
        for plane in range(depth):
            if count == 4 and cells[0].shape == outer.shape:
                logs = along_y(meta, cells[:3], plane, cells[3])
                held[0, plane], held[1, plane] = proximal(logs, outer[plane])
            elif count == 1:
                held[0, plane], held[1, plane] = proximal(cells[0][plane], outer[plane])
            else:
                for slot, part in enumerate(cells):
                    here = slot_rows(meta[0], slot, part.shape[1])
                    held[0, plane, here, :], held[1, plane, here, :] = proximal(part[plane], outer[plane, here, :])
            for k, out in enumerate(outs):
                copies.append(
                    pltpu.make_async_copy(
                        held.at[k, plane], out.at[plane, :, pl.ds(column, width)], sems.at[2 * (at * depth + plane) + k]
                    )
                )
                copies[-1].start()
    for copy in copies:
        copy.wait()


def final(pieces, external, meta, before):
    depth, rows, length = external.shape
    operands, kinds, scratch, size = [], [], [], 0
    for given, mine, start in pieces:
        width = given[0][0].shape[2]
        place = lambda i, m, mine=mine, start=start, width=width: (0, 0, ((m[3] if mine else 1 - m[3]) * (length // 2) + start) // width)
        operands += given + [(external, pl.BlockSpec((depth, rows, width), place))]
        kinds.append((len(given), mine, start))
        scratch.append(pltpu.VMEM((2, depth, rows, width), jnp.float32))
        size += depth * rows * width
    aliases = {1 + len(operands) + i: i for i in range(len(before))}
    operands += [(array, pl.BlockSpec(memory_space=pltpu.HBM)) for array in before]
    return call(
        functools.partial(final_kernel, kinds), "proximal", meta, operands, [external.shape] * 2, (20 * size, 6 * size),
        aliases, scratch + [pltpu.SemaphoreType.DMA((2 * depth * len(pieces),))], in_place=True,
    )


def own_planes(arrays, depth):
    return [(array, pl.BlockSpec((depth,) + array.shape[1:], lambda i, m: (0, 0, 0))) for array in arrays]


def pairs(count, first):
    ends = [(i, i + 1) for i in range(first, count - 1, 2)]
    return ends + [(j, i) for i, j in ends]


def neighbours(cells):
    count = lax.axis_size("gy")
    return lax.ppermute(cells, "gy", pairs(count, 0)), cells, lax.ppermute(cells, "gy", pairs(count, 1))


def row_meta():
    place, count = lax.axis_index("gy"), lax.axis_size("gy")
    odd = place % 2
    return [place + 1 - odd >= count, (place == 0) | (place + odd >= count), odd]


def swap(cells, bits):
    return lax.ppermute(cells, "gz", [(i, i ^ bits) for i in range(lax.axis_size("gz"))])


def exchange(parts):
    order = sorted(range(1, len(parts)), key=lambda r: -bin(r).count("1"))
    moved = dict((r, swap(parts[r], 2 * r)) for r in order)
    return [parts[0]] + [moved[r] for r in range(1, len(parts))]


def in_parts(potential, external):
    slots = lax.axis_size("gz")
    depth, rows, length = potential.shape
    parts = slots // 2
    place = lax.axis_index("gz")
    first_missing, second_missing, odd = row_meta()
    meta = jnp.stack([place // 2, first_missing, second_missing, place % 2, odd]).astype(jnp.int32)
    table = z_table(place, slots, depth)

    width = length // 4
    first = along_x(potential, meta, False, 0, width, 0, far=True)[0]
    later = along_x(potential, meta, False, width, width, 0, after=[first])[0]
    first = along_x(potential, meta, True, 0, width, 0, swap(first, 1))[0]
    later = along_x(potential, meta, True, width, width, parts, swap(later, 1), after=[first])

    first = neighbours(first)
    later = exchange(later)
    later = along_z(later, table, meta)
    first = along_y_parts(first, meta, parts)
    later = join(exchange(later), meta, after=first)
    later = neighbours(later)
    first = exchange(first)
    first = along_z(first, table, meta)
    later_other = swap(along_y_send(later, meta, depth, after=first), 1)
    first = exchange(first)

    outs = final([(y_operands(later, depth), True, width)], external, meta, [])
    first_other = swap(join(first, meta, depth, after=outs, after_far=True), 1)
    other = (own_planes([later_other], depth), False, width)
    own = (own_planes(first, depth), True, 0)
    outs = final([other, own], external, meta, outs)
    return tuple(final([(own_planes([first_other], depth), False, 0)], external, meta, outs))


def whole(potential, external):
    depth = RADIUS
    slots = lax.axis_size("gz")
    position, devices = lax.axis_index("gy"), lax.axis_size("gy")
    planes, rows, length = potential.shape

    def table(in_index, out_index):
        apart = in_index[:, None] - out_index[None, :]
        distance = apart.astype(jnp.float32)
        values = jnp.exp(-2.0 * distance * distance / float(RADIUS * RADIUS))
        return jnp.where(jnp.abs(apart) <= RADIUS, values, 0.0)

    def summed(equation, window, axis, kernel):
        highest_value = jnp.max(window, axis=axis, keepdims=True)
        weights = jnp.exp(window - highest_value)
        return jnp.log(jnp.einsum(equation, weights, kernel, precision=HIGHEST)) + highest_value

    border = jnp.full((planes, rows, depth), -jnp.inf, jnp.float32)
    padded = jnp.concatenate([border, potential, border], axis=-1)
    pieces = padded.reshape(planes, rows, length // BLOCK + 1, BLOCK)
    window = jnp.concatenate([pieces[..., :-1, :], pieces[..., 1:, :]], axis=-1)
    kernel = table(jnp.arange(2 * BLOCK) - depth, jnp.arange(BLOCK))
    logs = summed("...w,wo->...o", window, -1, kernel).reshape(potential.shape)

    paired, _, other = neighbours(logs)
    up, down = jnp.where(position % 2 == 0, other, paired), jnp.where(position % 2 == 0, paired, other)
    up = jnp.where(position == 0, -jnp.inf, up[:, rows - depth :])
    down = jnp.where(position == devices - 1, -jnp.inf, down[:, :depth])
    window = jnp.concatenate([up, logs, down], axis=1)
    kernel = table(jnp.arange(rows + 2 * depth) - depth, jnp.arange(rows))
    logs = summed("zwx,wo->zox", window, 1, kernel)

    logs = lax.all_to_all(logs, "gz", split_axis=1, concat_axis=0, tiled=True)
    cells = jnp.arange(slots * planes)
    logs = summed("wyx,wo->oyx", logs, 0, table(cells, cells))
    logs = lax.all_to_all(logs, "gz", split_axis=0, concat_axis=1, tiled=True)
    return proximal(logs, external)


def local(potential, external):
    slots = lax.axis_size("gz")
    depth, rows, length = potential.shape
    tiles = slots > 2 and slots & (slots - 1) == 0 and rows % (4 * slots) == 0 and slots * depth <= 32
    if tiles and rows == RADIUS and length % (4 * BLOCK) == 0:
        return in_parts(potential, external)
    return whole(potential, external)


def solution(mesh):
    return jax.shard_map(
        local,
        mesh=mesh,
        in_specs=(P("gz", "gy", None), P("gz", "gy", None)),
        out_specs=(P("gz", "gy", None), P("gz", "gy", None)),
        check_vma=False,
    )
```

time: 277 us -> 103 us (0.37)
  waiting for transfers between devices: 166 us -> 51.3 us
  local copies, waits for them, and re-layouts: 37.4 us -> 0.23 us
  matrix products: 36.1 us -> 0 us
  Pallas kernels: 0 us -> 25.1 us
  other arithmetic: 8.76 us -> 0.23 us
    all_to_all x4 -> x0, waiting for transfers between devices: 111 us -> none  [the longest x1 42.7 us: local(): lax.all_to_all(along_y, 'gz', split_axis=1, concat_axis=0, tiled=True)]
    dot_general x3 -> x0, matrix products: 36.1 us -> none  [the longest x1 13.1 us: along_middle(): summed = jnp.einsum('zwx,wo->zox', weights, kernel_table, precision=HIGHEST)]
    pallas_call x0 -> x13, Pallas kernels: none -> 25.1 us  [call(): pl.pallas_call(body, grid_spec=pltpu.PrefetchScalarGridSpec(num_scalar_pr...]
    all_to_all x4 -> x0, starting transfers between devices: 17.7 us -> none  [the longest x1 4.77 us: local(): lax.all_to_all(along_y, 'gz', split_axis=1, concat_axis=0, tiled=True)]
    ppermute x2 -> x20, starting transfers between devices: 8.6 us -> 25.2 us  [the longest x16 15.3 us: swap(): lax.ppermute(cells, 'gz', [(i, i ^ bits) for i in range(lax.axis_size('gz...]
    all_to_all x4 -> x0, local copies, waits for them, and re-layouts: 9.99 us -> none  [the longest x2 4.22 us: local(): lax.all_to_all(along_y, 'gz', split_axis=1, concat_axis=0, tiled=True)]
    unnamed x4 -> x10, local copies, waits for them, and re-layouts: 10 us -> 0.14 us
    sub x2 -> x0, local copies, waits for them, and re-layouts: 8.88 us -> none  [the longest x1 5.4 us: proximal(): log_level - (log_level + exp_level - shifted) / (1.0 + exp_level)]
  transfers between devices with their start and end apart: 6 -> 20, of which waited for: 5 -> 8; matrix products, arithmetic and copies ran while one was open for 15% -> 0% of each run, Pallas kernels for 0% -> 19%
where the time goes in v2:
time: 103 us
  waiting for transfers between devices  51.3 us (50%)
  starting transfers between devices  25.2 us (24%)
  Pallas kernels  25.1 us (24%)
    ppermute x16, waiting for transfers between devices, swap(): lax.ppermute(cells, 'gz', [(i, i ^ bits) for i in range(lax.axis_size('gz...  35.4 us
    pallas_call x13, Pallas kernels, call(): pl.pallas_call(body, grid_spec=pltpu.PrefetchScalarGridSpec(num_scalar_pr...  25.1 us
    ppermute x2, waiting for transfers between devices, neighbours(): lax.ppermute(cells, 'gy', pairs(count, 0))  15.9 us
    ppermute x16, starting transfers between devices, swap(): lax.ppermute(cells, 'gz', [(i, i ^ bits) for i in range(lax.axis_size('gz...  15.3 us
    ppermute x2, starting transfers between devices, neighbours(): lax.ppermute(cells, 'gy', pairs(count, 0))  8.03 us
  transfers between devices with their start and end apart: 20, of which 8 were waited for; matrix products, arithmetic and copies ran while one was open for 0% of the time, Pallas kernels for 19%

profile of v2, /device:TPU:0, one launch (start us, length us, event | category | flops | bytes accessed | tf_op | source)
XLA Modules:
  0.0 103.0 jit_solution(1659033329247589230)
XLA Ops:
  0.8 3.1 %along_x.4.refs_6_ = f32[3,128,512]{2,1,0:T(8,128)S(1)} custom-call(s32[5]{0:T(128)S(1)} %stack.31.refs_0_, f32[3,128,2048]{2,1,0:T(8,128)} %refs_3_.7, f32[3,128,2048]{2,1,0:T(8,128)} %refs_3_.7, f32[3,128,2048]{2,1,0:T(8,128)} %refs_3_.7, bf16[512,256]{1,0:T(8,128)(2,1)} %constant.101.clone.refs_4_, bf16[512,256]{1,0:T(8,128)(2,1)} %constant.102.clone.refs_5_), custom_call_target="tpu_custom_call" | custom-call | flops 603979776 | bytes 1572864 | tf_op jit(solution)/shard_map/along_x/pallas_call | solution.py:102
  4.4 1.5 %along_x.6 = f32[3,128,512]{2,1,0:T(8,128)S(1)} custom-call(s32[5]{0:T(128)S(1)} %stack.31.refs_0_, f32[3,128,2048]{2,1,0:T(8,128)S(1)} %copy-done, f32[3,128,2048]{2,1,0:T(8,128)S(1)} %copy-done, f32[3,128,2048]{2,1,0:T(8,128)S(1)} %copy-done, bf16[512,256]{1,0:T(8,128)(2,1)S(1)} %copy-done.3, bf16[512,256]{1,0:T(8,128)(2,1)S(1)} %copy-done.2, ...), custom_call_target="tpu_custom_call" | custom-call | flops 603979776 | bytes 1572864 | tf_op jit(solution)/shard_map/along_x/pallas_call | solution.py:102
  6.3 1.5 %along_x.5.refs_2_.refs_7_ = f32[6,128,512]{2,1,0:T(8,128)S(1)} custom-call(s32[5]{0:T(128)S(1)} %stack.31.refs_0_, f32[3,128,2048]{2,1,0:T(8,128)S(1)} %copy-done, f32[3,128,2048]{2,1,0:T(8,128)S(1)} %copy-done, f32[3,128,2048]{2,1,0:T(8,128)S(1)} %copy-done, bf16[512,256]{1,0:T(8,128)(2,1)S(1)} %copy-done.3, bf16[512,256]{1,0:T(8,128)(2,1)S(1)} %copy-done.2, ...), custom_call_target="tpu_custom_call" | custom-call | flops 603979776 | bytes 3145728 | tf_op jit(solution)/shard_map/along_x/pallas_call | solution.py:102
  8.7 5.7 %collective-permute-start.1 = (f32[6,128,512]{2,1,0:T(8,128)S(1)}, f32[6,128,512]{2,1,0:T(8,128)S(1)}, u32[]{:S(2)}, u32[]{:S(2)}) collective-permute-start(f32[6,128,512]{2,1,0:T(8,128)S(1)} %along_x.5.refs_2_.refs_7_), channel_id=1, source_target_pairs={{0,1},{2,3},{1,0},{3,2},{4,5},{6,7},{5,4},{7,6},{8,9},{10,11},{9,8... | collective-permute-start | bytes 4718600 | tf_op jit(solution)/shard_map/ppermute | solution.py:348
  14.5 1.5 %along_x.7 = (f32[6,32,512]{2,1,0:T(8,128)S(1)}, f32[6,32,512]{2,1,0:T(8,128)S(1)}, f32[6,32,512]{2,1,0:T(8,128)S(1)}, f32[6,32,512]{2,1,0:T(8,128)S(1)}) custom-call(s32[5]{0:T(128)S(1)} %stack.31.refs_0_, f32[3,128,2048]{2,1,0:T(8,128)S(1)} %copy-done, f32[3,128,2048]{2,1,0:T(8,128)S(1)} %copy-done, f32[3,128,2048]{2,1,0:T(8,128)S(1)} %copy-done, ...), custom_call_target="tpu_custom_call" | custom-call | flops 603979776 | bytes 3145728 | tf_op jit(solution)/shard_map/along_x/pallas_call | solution.py:102
  16.0 1.6 %collective-permute-start.10 = (f32[6,32,512]{2,1,0:T(8,128)S(1)}, f32[6,32,512]{2,1,0:T(8,128)S(1)}, u32[]{:S(2)}, u32[]{:S(2)}) collective-permute-start(f32[6,32,512]{2,1,0:T(8,128)S(1)} %get-tuple-element.31), channel_id=1, source_target_pairs={{0,8},{4,12},{8,0},{12,4},{16,24},{20,28},{24,16},{28,20},{1,9},{5... | collective-permute-start | bytes 1179656 | tf_op jit(solution)/shard_map/ppermute | solution.py:358
  17.6 1.5 %collective-permute-start.11 = (f32[6,32,512]{2,1,0:T(8,128)S(1)}, f32[6,32,512]{2,1,0:T(8,128)S(1)}, u32[]{:S(2)}, u32[]{:S(2)}) collective-permute-start(f32[6,32,512]{2,1,0:T(8,128)S(1)} %get-tuple-element.32), channel_id=1, source_target_pairs={{0,16},{4,20},{8,24},{12,28},{16,0},{20,4},{24,8},{28,12},{1,17},{... | collective-permute-start | bytes 1179656 | tf_op jit(solution)/shard_map/ppermute | solution.py:358
  19.8 8.3 %collective-permute-done.10.refs_3_ = f32[6,32,512]{2,1,0:T(8,128)S(1)} collective-permute-done((f32[6,32,512]{2,1,0:T(8,128)S(1)}, f32[6,32,512]{2,1,0:T(8,128)S(1)}, u32[]{:S(2)}, u32[]{:S(2)}) %collective-permute-start.10) | collective-permute-done | bytes 393248 | tf_op jit(solution)/shard_map/ppermute | solution.py:358
  28.1 8.2 %collective-permute-done.11.refs_4_ = f32[6,32,512]{2,1,0:T(8,128)S(1)} collective-permute-done((f32[6,32,512]{2,1,0:T(8,128)S(1)}, f32[6,32,512]{2,1,0:T(8,128)S(1)}, u32[]{:S(2)}, u32[]{:S(2)}) %collective-permute-start.11) | collective-permute-done | bytes 393248 | tf_op jit(solution)/shard_map/ppermute | solution.py:358
  36.3 1.5 %along_z.3 = (f32[6,32,512]{2,1,0:T(8,128)S(1)}, f32[6,32,512]{2,1,0:T(8,128)S(1)}, f32[6,32,512]{2,1,0:T(8,128)S(1)}, f32[6,32,512]{2,1,0:T(8,128)S(1)}) custom-call(s32[5]{0:T(128)S(1)} %stack.31.refs_0_, bf16[384,192]{1,0:T(8,128)(2,1)S(1)} %pad_maximum_fusion.refs_1_, f32[6,32,512]{2,1,0:T(8,128)S(1)} %get-tuple-element.30.refs_2_, ...), custom_call_target="tpu_custom_call" | custom-call | flops 603979776 | bytes 3145728 | tf_op jit(solution)/shard_map/along_z/pallas_call | solution.py:102
  41.3 7.5 %collective-permute-done.1.refs_1_ = f32[6,128,512]{2,1,0:T(8,128)S(1)} collective-permute-done((f32[6,128,512]{2,1,0:T(8,128)S(1)}, f32[6,128,512]{2,1,0:T(8,128)S(1)}, u32[]{:S(2)}, u32[]{:S(2)}) %collective-permute-start.1) | collective-permute-done | bytes 1572896 | tf_op jit(solution)/shard_map/ppermute | solution.py:348
  48.9 2.8 %along_y.2 = (f32[6,32,512]{2,1,0:T(8,128)S(1)}, f32[6,32,512]{2,1,0:T(8,128)S(1)}, f32[6,32,512]{2,1,0:T(8,128)S(1)}, f32[6,32,512]{2,1,0:T(8,128)S(1)}) custom-call(s32[5]{0:T(128)S(1)} %stack.31.refs_0_, f32[6,128,512]{2,1,0:T(8,128)S(1)} %collective-permute-done.1.refs_1_, f32[6,128,512]{2,1,0:T(8,128)S(1)} %along_x.5.refs_2_.refs_7_, ...), custom_call_target="tpu_custom_call" | custom-call | flops 1207959552 | bytes 3145728 | tf_op jit(solution)/shard_map/along_y/pallas_call | solution.py:102
  51.7 5.2 %collective-permute-done.14.refs_3_ = f32[6,32,512]{2,1,0:T(8,128)S(1)} collective-permute-done((f32[6,32,512]{2,1,0:T(8,128)S(1)}, f32[6,32,512]{2,1,0:T(8,128)S(1)}, u32[]{:S(2)}, u32[]{:S(2)}) %collective-permute-start.14) | collective-permute-done | bytes 393248 | tf_op jit(solution)/shard_map/ppermute | solution.py:358
  58.5 2.3 %collective-permute-start.16 = (f32[6,128,512]{2,1,0:T(8,128)S(1)}, f32[6,128,512]{2,1,0:T(8,128)S(1)}, u32[]{:S(2)}, u32[]{:S(2)}) collective-permute-start(f32[6,128,512]{2,1,0:T(8,128)S(1)} %join.2.refs_2_), channel_id=1, source_target_pairs={{0,1},{2,3},{1,0},{3,2},{4,5},{6,7},{5,4},{7,6},{8,9},{10,11},{9,8... | collective-permute-start | bytes 4718600 | tf_op jit(solution)/shard_map/ppermute | solution.py:348
  62.6 1.8 %collective-permute-start.5 = (f32[6,32,512]{2,1,0:T(8,128)S(1)}, f32[6,32,512]{2,1,0:T(8,128)S(1)}, u32[]{:S(2)}, u32[]{:S(2)}) collective-permute-start(f32[6,32,512]{2,1,0:T(8,128)S(1)} %get-tuple-element.25.refs_8_), channel_id=1, source_target_pairs={{0,24},{4,28},{8,16},{12,20},{16,8},{20,12},{24,0},{28,4},{1,25},{... | collective-permute-start | bytes 1179656 | tf_op jit(solution)/shard_map/ppermute | solution.py:358
  64.3 7.6 %collective-permute-done.3.refs_3_ = f32[6,32,512]{2,1,0:T(8,128)S(1)} collective-permute-done((f32[6,32,512]{2,1,0:T(8,128)S(1)}, f32[6,32,512]{2,1,0:T(8,128)S(1)}, u32[]{:S(2)}, u32[]{:S(2)}) %collective-permute-start.3) | collective-permute-done | bytes 393248 | tf_op jit(solution)/shard_map/ppermute | solution.py:358
  71.9 5.7 %collective-permute-done.4.refs_4_ = f32[6,32,512]{2,1,0:T(8,128)S(1)} collective-permute-done((f32[6,32,512]{2,1,0:T(8,128)S(1)}, f32[6,32,512]{2,1,0:T(8,128)S(1)}, u32[]{:S(2)}, u32[]{:S(2)}) %collective-permute-start.4) | collective-permute-done | bytes 393248 | tf_op jit(solution)/shard_map/ppermute | solution.py:358
  77.6 1.4 %along_z.2 = (f32[6,32,512]{2,1,0:T(8,128)S(1)}, f32[6,32,512]{2,1,0:T(8,128)S(1)}, f32[6,32,512]{2,1,0:T(8,128)S(1)}, f32[6,32,512]{2,1,0:T(8,128)S(1)}) custom-call(s32[5]{0:T(128)S(1)} %stack.31.refs_0_, bf16[384,192]{1,0:T(8,128)(2,1)S(1)} %pad_maximum_fusion.refs_1_, f32[6,32,512]{2,1,0:T(8,128)S(1)} %get-tuple-element.22.refs_2_.refs_5_, ...), custom_call_target="tpu_custom_call" | custom-call | flops 603979776 | bytes 3145728 | tf_op jit(solution)/shard_map/along_z/pallas_call | solution.py:102
  79.1 1.5 %collective-permute-start.6 = (f32[6,32,512]{2,1,0:T(8,128)S(1)}, f32[6,32,512]{2,1,0:T(8,128)S(1)}, u32[]{:S(2)}, u32[]{:S(2)}) collective-permute-start(f32[6,32,512]{2,1,0:T(8,128)S(1)} %get-tuple-element.27.refs_6_), channel_id=1, source_target_pairs={{0,8},{4,12},{8,0},{12,4},{16,24},{20,28},{24,16},{28,20},{1,9},{5... | collective-permute-start | bytes 1179656 | tf_op jit(solution)/shard_map/ppermute | solution.py:358
  82.6 8.4 %collective-permute-done.16.refs_1_ = f32[6,128,512]{2,1,0:T(8,128)S(1)} collective-permute-done((f32[6,128,512]{2,1,0:T(8,128)S(1)}, f32[6,128,512]{2,1,0:T(8,128)S(1)}, u32[]{:S(2)}, u32[]{:S(2)}) %collective-permute-start.16) | collective-permute-done | bytes 1572896 | tf_op jit(solution)/shard_map/ppermute | solution.py:348
  91.0 1.7 %along_y.3 = f32[3,128,512]{2,1,0:T(8,128)S(1)} custom-call(s32[5]{0:T(128)S(1)} %stack.31.refs_0_, f32[6,128,512]{2,1,0:T(8,128)S(1)} %collective-permute-done.16.refs_1_, f32[6,128,512]{2,1,0:T(8,128)S(1)} %join.2.refs_2_, f32[6,128,512]{2,1,0:T(8,128)S(1)} %collective-permute-done.17.refs_3_, bf16[512,384]{1,0:T(8,128)(2,1)S(1)} %copy-done.4, ...), custom_call_target="tpu_custom_call" | custom-call | flops 603979776 | bytes 1572864 | tf_op jit(solution)/shard_map/along_y/pallas_call | solution.py:102
  92.9 3.4 %proximal.3 = (f32[3,128,2048]{2,1,0:T(8,128)}, f32[3,128,2048]{2,1,0:T(8,128)}) custom-call(s32[5]{0:T(128)S(1)} %stack.31.refs_0_, f32[6,128,512]{2,1,0:T(8,128)S(1)} %collective-permute-done.16.refs_1_, f32[6,128,512]{2,1,0:T(8,128)S(1)} %join.2.refs_2_, f32[6,128,512]{2,1,0:T(8,128)S(1)} %collective-permute-done.17.refs_3_, ...), custom_call_target="tpu_custom_call" | custom-call | flops 7864320 | bytes 12582912 | tf_op jit(solution)/shard_map/proximal/pallas_call | solution.py:102
  97.4 3.3 %proximal.4 = (f32[3,128,2048]{2,1,0:T(8,128)}, f32[3,128,2048]{2,1,0:T(8,128)}) custom-call(s32[5]{0:T(128)S(1)} %stack.31.refs_0_, f32[3,128,512]{2,1,0:T(8,128)S(1)} %collective-permute-done.19.refs_1_, f32[3,128,2048]{2,1,0:T(8,128)S(1)} %copy-done.1, ...), custom_call_target="tpu_custom_call", output_to_operand_aliasing={{0}: (8, {}), {1}: (9, {})} | custom-call | flops 15728640 | bytes 12582912 | tf_op jit(solution)/shard_map/proximal/pallas_call | solution.py:102
  100.7 2.2 %proximal.5 = (f32[3,128,2048]{2,1,0:T(8,128)}, f32[3,128,2048]{2,1,0:T(8,128)}) custom-call(s32[5]{0:T(128)S(1)} %stack.31.refs_0_, f32[3,128,512]{2,1,0:T(8,128)S(1)} %collective-permute-done.18.refs_1_, f32[3,128,2048]{2,1,0:T(8,128)S(1)} %copy-done.1, f32[3,128,2048]{2,1,0:T(8,128)} %get-tuple-element.40.refs_3_, ...), custom_call_target="tpu_custom_call", output_to_operand_aliasing={{0}: (3, {}), {1}: (4, {})} | custom-call | flops 7864320 | bytes 12582912 | tf_op jit(solution)/shard_map/proximal/pallas_call | solution.py:102
  (43 shorter events, 12.8 us)
Async XLA Ops:
  0.8 3.6 %copy-start = (f32[3,128,2048]{2,1,0:T(8,128)S(1)}, f32[3,128,2048]{2,1,0:T(8,128)}, u32[]{:S(2)}) copy-start(f32[3,128,2048]{2,1,0:T(8,128)} %refs_3_.7) | copy-start | bytes 9437188
  0.8 3.6 %copy-start.2 = (bf16[512,256]{1,0:T(8,128)(2,1)S(1)}, bf16[512,256]{1,0:T(8,128)(2,1)}, u32[]{:S(2)}) copy-start(bf16[512,256]{1,0:T(8,128)(2,1)} %constant.102.clone.refs_5_) | copy-start | bytes 786436
  0.8 3.6 %copy-start.3 = (bf16[512,256]{1,0:T(8,128)(2,1)S(1)}, bf16[512,256]{1,0:T(8,128)(2,1)}, u32[]{:S(2)}) copy-start(bf16[512,256]{1,0:T(8,128)(2,1)} %constant.101.clone.refs_4_) | copy-start | bytes 786436
  3.9 2.4 %collective-permute-start = (f32[3,128,512]{2,1,0:T(8,128)S(1)}, f32[3,128,512]{2,1,0:T(8,128)S(1)}, u32[]{:S(2)}, u32[]{:S(2)}) collective-permute-start(f32[3,128,512]{2,1,0:T(8,128)S(1)} %along_x.4.refs_6_), channel_id=1, source_target_pairs={{0,4},{4,0},{8,12},{12,8},{16,20},{20,16},{24,28},{28,24},{1,5},{5... | collective-permute-start | bytes 2359304 | tf_op jit(solution)/shard_map/ppermute | solution.py:358
  5.9 8.6 %collective-permute-start.9 = (f32[3,128,512]{2,1,0:T(8,128)S(1)}, f32[3,128,512]{2,1,0:T(8,128)S(1)}, u32[]{:S(2)}, u32[]{:S(2)}) collective-permute-start(f32[3,128,512]{2,1,0:T(8,128)S(1)} %along_x.6), channel_id=1, source_target_pairs={{0,4},{4,0},{8,12},{12,8},{16,20},{20,16},{24,28},{28,24},{1,5},{5... | collective-permute-start | bytes 2359304 | tf_op jit(solution)/shard_map/ppermute | solution.py:358
  7.8 41.1 %copy-start.4 = (bf16[512,384]{1,0:T(8,128)(2,1)S(1)}, bf16[512,384]{1,0:T(8,128)(2,1)}, u32[]{:S(2)}) copy-start(bf16[512,384]{1,0:T(8,128)(2,1)} %constant.103.clone.refs_4_) | copy-start | bytes 1179652
  7.8 33.5 %collective-permute-start.2 = (f32[6,128,512]{2,1,0:T(8,128)S(1)}, f32[6,128,512]{2,1,0:T(8,128)S(1)}, u32[]{:S(2)}, u32[]{:S(2)}) collective-permute-start(f32[6,128,512]{2,1,0:T(8,128)S(1)} %along_x.5.refs_2_.refs_7_), channel_id=1, source_target_pairs={{1,2},{2,1},{5,6},{6,5},{9,10},{10,9},{13,14},{14,13},{17,18},{18,... | collective-permute-start | bytes 4718600 | tf_op jit(solution)/shard_map/ppermute | solution.py:348
  8.7 40.2 %collective-permute-start.1 = (f32[6,128,512]{2,1,0:T(8,128)S(1)}, f32[6,128,512]{2,1,0:T(8,128)S(1)}, u32[]{:S(2)}, u32[]{:S(2)}) collective-permute-start(f32[6,128,512]{2,1,0:T(8,128)S(1)} %along_x.5.refs_2_.refs_7_), channel_id=1, source_target_pairs={{0,1},{2,3},{1,0},{3,2},{4,5},{6,7},{5,4},{7,6},{8,9},{10,11},{9,8... | collective-permute-start | bytes 4718600 | tf_op jit(solution)/shard_map/ppermute | solution.py:348
  16.0 12.1 %collective-permute-start.10 = (f32[6,32,512]{2,1,0:T(8,128)S(1)}, f32[6,32,512]{2,1,0:T(8,128)S(1)}, u32[]{:S(2)}, u32[]{:S(2)}) collective-permute-start(f32[6,32,512]{2,1,0:T(8,128)S(1)} %get-tuple-element.31), channel_id=1, source_target_pairs={{0,8},{4,12},{8,0},{12,4},{16,24},{20,28},{24,16},{28,20},{1,9},{5... | collective-permute-start | bytes 1179656 | tf_op jit(solution)/shard_map/ppermute | solution.py:358
  17.6 18.8 %collective-permute-start.11 = (f32[6,32,512]{2,1,0:T(8,128)S(1)}, f32[6,32,512]{2,1,0:T(8,128)S(1)}, u32[]{:S(2)}, u32[]{:S(2)}) collective-permute-start(f32[6,32,512]{2,1,0:T(8,128)S(1)} %get-tuple-element.32), channel_id=1, source_target_pairs={{0,16},{4,20},{8,24},{12,28},{16,0},{20,4},{24,8},{28,12},{1,17},{... | collective-permute-start | bytes 1179656 | tf_op jit(solution)/shard_map/ppermute | solution.py:358
  19.1 17.2 %collective-permute-start.12 = (f32[6,32,512]{2,1,0:T(8,128)S(1)}, f32[6,32,512]{2,1,0:T(8,128)S(1)}, u32[]{:S(2)}, u32[]{:S(2)}) collective-permute-start(f32[6,32,512]{2,1,0:T(8,128)S(1)} %get-tuple-element.33), channel_id=1, source_target_pairs={{0,24},{4,28},{8,16},{12,20},{16,8},{20,12},{24,0},{28,4},{1,25},{... | collective-permute-start | bytes 1179656 | tf_op jit(solution)/shard_map/ppermute | solution.py:358
  37.8 13.9 %collective-permute-start.13 = (f32[6,32,512]{2,1,0:T(8,128)S(1)}, f32[6,32,512]{2,1,0:T(8,128)S(1)}, u32[]{:S(2)}, u32[]{:S(2)}) collective-permute-start(f32[6,32,512]{2,1,0:T(8,128)S(1)} %get-tuple-element.35), channel_id=1, source_target_pairs={{0,8},{4,12},{8,0},{12,4},{16,24},{20,28},{24,16},{28,20},{1,9},{5... | collective-permute-start | bytes 1179656 | tf_op jit(solution)/shard_map/ppermute | solution.py:358
  39.1 17.9 %collective-permute-start.14 = (f32[6,32,512]{2,1,0:T(8,128)S(1)}, f32[6,32,512]{2,1,0:T(8,128)S(1)}, u32[]{:S(2)}, u32[]{:S(2)}) collective-permute-start(f32[6,32,512]{2,1,0:T(8,128)S(1)} %get-tuple-element.36), channel_id=1, source_target_pairs={{0,16},{4,20},{8,24},{12,28},{16,0},{20,4},{24,8},{28,12},{1,17},{... | collective-permute-start | bytes 1179656 | tf_op jit(solution)/shard_map/ppermute | solution.py:358
  39.9 17.0 %collective-permute-start.15 = (f32[6,32,512]{2,1,0:T(8,128)S(1)}, f32[6,32,512]{2,1,0:T(8,128)S(1)}, u32[]{:S(2)}, u32[]{:S(2)}) collective-permute-start(f32[6,32,512]{2,1,0:T(8,128)S(1)} %get-tuple-element.37), channel_id=1, source_target_pairs={{0,24},{4,28},{8,16},{12,20},{16,8},{20,12},{24,0},{28,4},{1,25},{... | collective-permute-start | bytes 1179656 | tf_op jit(solution)/shard_map/ppermute | solution.py:358
  57.6 25.0 %collective-permute-start.17 = (f32[6,128,512]{2,1,0:T(8,128)S(1)}, f32[6,128,512]{2,1,0:T(8,128)S(1)}, u32[]{:S(2)}, u32[]{:S(2)}) collective-permute-start(f32[6,128,512]{2,1,0:T(8,128)S(1)} %join.2.refs_2_), channel_id=1, source_target_pairs={{1,2},{2,1},{5,6},{6,5},{9,10},{10,9},{13,14},{14,13},{17,18},{18,... | collective-permute-start | bytes 4718600 | tf_op jit(solution)/shard_map/ppermute | solution.py:348
  58.5 32.4 %collective-permute-start.16 = (f32[6,128,512]{2,1,0:T(8,128)S(1)}, f32[6,128,512]{2,1,0:T(8,128)S(1)}, u32[]{:S(2)}, u32[]{:S(2)}) collective-permute-start(f32[6,128,512]{2,1,0:T(8,128)S(1)} %join.2.refs_2_), channel_id=1, source_target_pairs={{0,1},{2,3},{1,0},{3,2},{4,5},{6,7},{5,4},{7,6},{8,9},{10,11},{9,8... | collective-permute-start | bytes 4718600 | tf_op jit(solution)/shard_map/ppermute | solution.py:348
  60.8 11.1 %collective-permute-start.3 = (f32[6,32,512]{2,1,0:T(8,128)S(1)}, f32[6,32,512]{2,1,0:T(8,128)S(1)}, u32[]{:S(2)}, u32[]{:S(2)}) collective-permute-start(f32[6,32,512]{2,1,0:T(8,128)S(1)} %get-tuple-element.23.refs_6_), channel_id=1, source_target_pairs={{0,8},{4,12},{8,0},{12,4},{16,24},{20,28},{24,16},{28,20},{1,9},{5... | collective-permute-start | bytes 1179656 | tf_op jit(solution)/shard_map/ppermute | solution.py:358
  61.4 16.2 %collective-permute-start.4 = (f32[6,32,512]{2,1,0:T(8,128)S(1)}, f32[6,32,512]{2,1,0:T(8,128)S(1)}, u32[]{:S(2)}, u32[]{:S(2)}) collective-permute-start(f32[6,32,512]{2,1,0:T(8,128)S(1)} %get-tuple-element.24.refs_7_), channel_id=1, source_target_pairs={{0,16},{4,20},{8,24},{12,28},{16,0},{20,4},{24,8},{28,12},{1,17},{... | collective-permute-start | bytes 1179656 | tf_op jit(solution)/shard_map/ppermute | solution.py:358
  62.6 15.0 %collective-permute-start.5 = (f32[6,32,512]{2,1,0:T(8,128)S(1)}, f32[6,32,512]{2,1,0:T(8,128)S(1)}, u32[]{:S(2)}, u32[]{:S(2)}) collective-permute-start(f32[6,32,512]{2,1,0:T(8,128)S(1)} %get-tuple-element.25.refs_8_), channel_id=1, source_target_pairs={{0,24},{4,28},{8,16},{12,20},{16,8},{20,12},{24,0},{28,4},{1,25},{... | collective-permute-start | bytes 1179656 | tf_op jit(solution)/shard_map/ppermute | solution.py:358
  79.1 17.2 %collective-permute-start.6 = (f32[6,32,512]{2,1,0:T(8,128)S(1)}, f32[6,32,512]{2,1,0:T(8,128)S(1)}, u32[]{:S(2)}, u32[]{:S(2)}) collective-permute-start(f32[6,32,512]{2,1,0:T(8,128)S(1)} %get-tuple-element.27.refs_6_), channel_id=1, source_target_pairs={{0,8},{4,12},{8,0},{12,4},{16,24},{20,28},{24,16},{28,20},{1,9},{5... | collective-permute-start | bytes 1179656 | tf_op jit(solution)/shard_map/ppermute | solution.py:358
  80.6 15.7 %collective-permute-start.7 = (f32[6,32,512]{2,1,0:T(8,128)S(1)}, f32[6,32,512]{2,1,0:T(8,128)S(1)}, u32[]{:S(2)}, u32[]{:S(2)}) collective-permute-start(f32[6,32,512]{2,1,0:T(8,128)S(1)} %get-tuple-element.28.refs_7_), channel_id=1, source_target_pairs={{0,16},{4,20},{8,24},{12,28},{16,0},{20,4},{24,8},{28,12},{1,17},{... | collective-permute-start | bytes 1179656 | tf_op jit(solution)/shard_map/ppermute | solution.py:358
  81.2 15.1 %collective-permute-start.8 = (f32[6,32,512]{2,1,0:T(8,128)S(1)}, f32[6,32,512]{2,1,0:T(8,128)S(1)}, u32[]{:S(2)}, u32[]{:S(2)}) collective-permute-start(f32[6,32,512]{2,1,0:T(8,128)S(1)} %get-tuple-element.29.refs_8_), channel_id=1, source_target_pairs={{0,24},{4,28},{8,16},{12,20},{16,8},{20,12},{24,0},{28,4},{1,25},{... | collective-permute-start | bytes 1179656 | tf_op jit(solution)/shard_map/ppermute | solution.py:358
  92.7 4.7 %collective-permute-start.19 = (f32[3,128,512]{2,1,0:T(8,128)S(1)}, f32[3,128,512]{2,1,0:T(8,128)S(1)}, u32[]{:S(2)}, u32[]{:S(2)}) collective-permute-start(f32[3,128,512]{2,1,0:T(8,128)S(1)} %along_y.3), channel_id=1, source_target_pairs={{0,4},{4,0},{8,12},{12,8},{16,20},{20,16},{24,28},{28,24},{1,5},{5... | collective-permute-start | bytes 2359304 | tf_op jit(solution)/shard_map/ppermute | solution.py:358
  96.9 3.8 %collective-permute-start.18 = (f32[3,128,512]{2,1,0:T(8,128)S(1)}, f32[3,128,512]{2,1,0:T(8,128)S(1)}, u32[]{:S(2)}, u32[]{:S(2)}) collective-permute-start(f32[3,128,512]{2,1,0:T(8,128)S(1)} %join.3), channel_id=1, source_target_pairs={{0,4},{4,0},{8,12},{12,8},{16,20},{20,16},{24,28},{28,24},{1,5},{5... | collective-permute-start | bytes 2359304 | tf_op jit(solution)/shard_map/ppermute | solution.py:358
  (1 other events, 1.9 us)

commit v3 on v2

--- a/solution.py
+++ b/solution.py
@@ -12,6 +12,7 @@
 RADIUS = 128
 BLOCK = 2 * RADIUS
 VMEM_BYTES = 24 * 1024 * 1024
+FIRST_CUTS, LATER_CUTS = 1, 1
 LOWEST = -1e30
 
 HIGHEST = lax.Precision.HIGHEST
@@ -83,6 +84,12 @@
 
 def slot_rows(place, slot, rows):
     return pl.ds(pl.multiple_of(lax.bitwise_xor(place, slot) * rows, rows), rows)
+
+
+def tiles(place, parts, rows):
+    part, width = parts[0].shape[1:]
+    count = rows // part
+    return [(slot_rows(place, at % count, part), pl.ds(at // count * width, width)) for at in range(len(parts))]
 
 
 def all_of(array):
@@ -139,15 +146,14 @@
         else:
             refs[0][own, :, columns] = result
     if parts:
-        for slot, out in enumerate(refs):
-            here = slot_rows(meta[0], slot, rows // parts)
-            out[own] = held[:, here, :]
-            out[depth:] = other[:, here, :]
+        for out, (here, columns) in zip(refs, tiles(meta[0], refs, rows)):
+            out[own] = held[:, here, columns]
+            out[depth:] = other[:, here, columns]
     elif received:
         refs[0][depth:] = other[...]
 
 
-def along_x(potential, meta, mine, start, width, parts, received=None, after=(), far=False):
+def along_x(potential, meta, mine, start, width, parts, received=None, cuts=1, after=(), far=False):
     depth, rows, length = potential.shape
     half = length // 2
 
@@ -169,7 +175,7 @@
     if received is not None:
         planes = 2 * depth
         operands.append((received, all_of(received)))
-    outs = [(planes, rows // parts, width)] * parts if parts else [(planes, rows, width)]
+    outs = [(planes, rows // parts, width // cuts)] * (parts * cuts) if parts else [(planes, rows, width)]
     count = depth * rows * width
     return call(
         functools.partial(x_kernel, edges, received is not None, parts),
@@ -204,14 +210,14 @@
     planes, rows, width = own.shape
     for plane in range(planes):
         held[plane] = along_y(meta, (paired, own, other), plane, table)
-    for slot, out in enumerate(outs):
-        out[...] = held[:, slot_rows(meta[0], slot, rows // len(outs)), :]
-
-
-def along_y_parts(cells, meta, parts, after=()):
+    for out, (here, columns) in zip(outs, tiles(meta[0], outs, rows)):
+        out[...] = held[:, here, columns]
+
+
+def along_y_parts(cells, meta, parts, cuts=1, after=()):
     planes, rows, width = cells[1].shape
     return call(
-        y_parts_kernel, "along_y", meta, y_operands(cells, planes), [(planes, rows // parts, width)] * parts,
+        y_parts_kernel, "along_y", meta, y_operands(cells, planes), [(planes, rows // parts, width // cuts)] * (parts * cuts),
         y_work(cells[1].size), scratch=[pltpu.VMEM((planes, rows, width), jnp.float32)], after=after,
     )
 
@@ -259,40 +265,40 @@
     return jnp.concatenate([high, values - high], axis=0).astype(jnp.bfloat16)
 
 
-def along_z(parts, table, meta):
+def along_z(parts, table, meta, after=(), weight=1):
     count = len(parts) * parts[0].size
     return call(
         z_kernel, "along_z", meta, [(array, all_of(array)) for array in [table] + parts], [part.shape for part in parts],
-        (768 * count, 2 * count),
+        (768 * count * weight, 2 * count), after=after,
     )
 
 
 def join_kernel(meta, *refs):
     ins, out = refs[:-1], refs[-1]
-    for slot, part in enumerate(ins):
-        out[:, slot_rows(meta[0], slot, part.shape[1]), :] = part[...]
-
-
-def join(parts, meta, first=0, after=(), after_far=False):
+    for part, (here, columns) in zip(ins, tiles(meta[0], ins, out.shape[1])):
+        out[:, here, columns] = part[...]
+
+
+def join(parts, meta, cuts, first=0, after=(), after_far=False):
     planes, part, width = parts[0].shape
     block = planes - first
     spec = pl.BlockSpec((block, part, width), lambda i, m: (first // block, 0, 0))
-    return call(
-        join_kernel, "join", meta, [(array, spec) for array in parts], [(block, part * len(parts), width)], (0, 0), after=after,
-        after_far=after_far,
+    shape = (block, part * len(parts) // cuts, width * cuts)
+    return call(
+        join_kernel, "join", meta, [(array, spec) for array in parts], [shape], (0, 0), after=after, after_far=after_far
     )[0]
 
 
 def final_kernel(pieces, meta, *refs):
     refs = list(refs)
     ins = [[refs.pop(0) for _ in range(count + 1)] for count, _, _ in pieces]
-    results, sems = refs[-1 - len(pieces) : -1], refs[-1]
+    held_in, sems = refs[-1 - len(pieces) : -1], refs[-1]
     outs = refs[-3 - len(pieces) : -1 - len(pieces)]
     depth = ins[0][-1].shape[0]
     half = outs[0].shape[2] // 2
     copies = []
     for at, (count, mine, start) in enumerate(pieces):
-        cells, outer, held = ins[at][:-1], ins[at][-1], results[at]
+        cells, outer, held = ins[at][:-1], ins[at][-1], held_in[at]
         width = outer.shape[2]
         column = pl.multiple_of((meta[3] if mine else 1 - meta[3]) * half + start, width)
         for plane in range(depth):
@@ -302,9 +308,9 @@
             elif count == 1:
                 held[0, plane], held[1, plane] = proximal(cells[0][plane], outer[plane])
             else:
-                for slot, part in enumerate(cells):
-                    here = slot_rows(meta[0], slot, part.shape[1])
-                    held[0, plane, here, :], held[1, plane, here, :] = proximal(part[plane], outer[plane, here, :])
+                for part, (here, columns) in zip(cells, tiles(meta[0], cells, outer.shape[1])):
+                    results = proximal(part[plane], outer[plane, here, columns])
+                    held[0, plane, here, columns], held[1, plane, here, columns] = results
             for k, out in enumerate(outs):
                 copies.append(
                     pltpu.make_async_copy(
@@ -319,8 +325,7 @@
 def final(pieces, external, meta, before):
     depth, rows, length = external.shape
     operands, kinds, scratch, size = [], [], [], 0
-    for given, mine, start in pieces:
-        width = given[0][0].shape[2]
+    for given, mine, start, width in pieces:
         place = lambda i, m, mine=mine, start=start, width=width: (0, 0, ((m[3] if mine else 1 - m[3]) * (length // 2) + start) // width)
         operands += given + [(external, pl.BlockSpec((depth, rows, width), place))]
         kinds.append((len(given), mine, start))
@@ -374,28 +379,33 @@
     table = z_table(place, slots, depth)
 
     width = length // 4
-    first = along_x(potential, meta, False, 0, width, 0, far=True)[0]
-    later = along_x(potential, meta, False, width, width, 0, after=[first])[0]
-    first = along_x(potential, meta, True, 0, width, 0, swap(first, 1))[0]
-    later = along_x(potential, meta, True, width, width, parts, swap(later, 1), after=[first])
+    later = along_x(potential, meta, False, width, width, 0, far=True)[0]
+    first = along_x(potential, meta, False, 0, width, 0, after=[later])[0]
+    later = along_x(potential, meta, True, width, width, parts, swap(later, 1))
+    first = along_x(potential, meta, True, 0, width, 0, swap(first, 1), after=later)[0]
+    own_first = first
+
+    def over_z(cells, cuts):
+        cells = [exchange(cells[i * parts : (i + 1) * parts]) for i in range(cuts)]
+        return [along_z(part, table, meta) for part in cells]
+
+    def back(cells):
+        return [part for parts in cells for part in exchange(parts)]
 
     first = neighbours(first)
-    later = exchange(later)
-    later = along_z(later, table, meta)
-    first = along_y_parts(first, meta, parts)
-    later = join(exchange(later), meta, after=first)
+    later = [along_z(exchange(later), table, meta, [own_first], 30)]
+    later = join(back(later), meta, LATER_CUTS)
+    first = along_y_parts(first, meta, parts, FIRST_CUTS, after=[later])
     later = neighbours(later)
-    first = exchange(first)
-    first = along_z(first, table, meta)
-    later_other = swap(along_y_send(later, meta, depth, after=first), 1)
-    first = exchange(first)
-
-    outs = final([(y_operands(later, depth), True, width)], external, meta, [])
-    first_other = swap(join(first, meta, depth, after=outs, after_far=True), 1)
-    other = (own_planes([later_other], depth), False, width)
-    own = (own_planes(first, depth), True, 0)
+    first = over_z(first, FIRST_CUTS)
+    given = swap(along_y_send(later, meta, depth, after=first[-1]), 1)
+    first = back(first)
+    outs = final([(y_operands(later, depth), True, width, width)], external, meta, [])
+    lent = swap(join(first, meta, FIRST_CUTS, depth, after=outs, after_far=True), 1)
+    other = (own_planes([given], depth), False, width, width)
+    own = (own_planes(first, depth), True, 0, width)
     outs = final([other, own], external, meta, outs)
-    return tuple(final([(own_planes([first_other], depth), False, 0)], external, meta, outs))
+    return tuple(final([(own_planes([lent], depth), False, 0, width)], external, meta, outs))
 
 
 def whole(potential, external):

time: 103 us -> 103 us (level)
  waiting for transfers between devices: 51.3 us -> 49.1 us
  starting transfers between devices: 25.2 us -> 26.8 us
    ppermute x2, waiting for transfers between devices: 15.9 us -> 7.13 us  [neighbours(): lax.ppermute(cells, 'gy', pairs(count, 0))]
    ppermute x16, waiting for transfers between devices: 35.4 us -> 41.9 us  [swap(): lax.ppermute(cells, 'gz', [(i, i ^ bits) for i in range(lax.axis_size('gz...]
    ppermute x2, starting transfers between devices: 8.03 us -> 9.19 us  [neighbours(): lax.ppermute(cells, 'gy', pairs(count, 0))]
  transfers between devices with their start and end apart: 20 -> 20, of which waited for: 8 -> 9; matrix products, arithmetic and copies ran while one was open for 0% -> 0% of each run, Pallas kernels for 19% -> 19%
where the time goes in v3:
time: 103 us; the launch traced here: 102 us
  waiting for transfers between devices  49.1 us (48%)
  starting transfers between devices  26.8 us (26%)
  Pallas kernels  25.1 us (24%)
  between operations  1.03 us (1%)
    ppermute x16, waiting for transfers between devices, swap(): lax.ppermute(cells, 'gz', [(i, i ^ bits) for i in range(lax.axis_size('gz...  41.9 us
    pallas_call x13, Pallas kernels, call(): pl.pallas_call(body, grid_spec=pltpu.PrefetchScalarGridSpec(num_scalar_pr...  25.1 us
    ppermute x16, starting transfers between devices, swap(): lax.ppermute(cells, 'gz', [(i, i ^ bits) for i in range(lax.axis_size('gz...  15.9 us
    ppermute x2, starting transfers between devices, neighbours(): lax.ppermute(cells, 'gy', pairs(count, 0))  9.19 us
    ppermute x2, waiting for transfers between devices, neighbours(): lax.ppermute(cells, 'gy', pairs(count, 0))  7.13 us
  transfers between devices with their start and end apart: 20, of which 9 were waited for; matrix products, arithmetic and copies ran while one was open for 0% of the time, Pallas kernels for 19%

profile of v3, /device:TPU:0, one launch (start us, length us, event | category | flops | bytes accessed | tf_op | source)
XLA Modules:
  0.0 102.5 jit_solution(10505827615015109387)
XLA Ops:
  0.8 3.1 %along_x.4.refs_6_ = f32[3,128,512]{2,1,0:T(8,128)S(1)} custom-call(s32[5]{0:T(128)S(1)} %stack.31.refs_0_, f32[3,128,2048]{2,1,0:T(8,128)} %refs_3_.7, f32[3,128,2048]{2,1,0:T(8,128)} %refs_3_.7, f32[3,128,2048]{2,1,0:T(8,128)} %refs_3_.7, bf16[512,256]{1,0:T(8,128)(2,1)} %constant.101.clone.refs_4_, bf16[512,256]{1,0:T(8,128)(2,1)} %constant.102.clone.refs_5_), custom_call_target="tpu_custom_call" | custom-call | flops 603979776 | bytes 1572864 | tf_op jit(solution)/shard_map/along_x/pallas_call | solution.py:109
  4.4 1.5 %along_x.5 = f32[3,128,512]{2,1,0:T(8,128)S(1)} custom-call(s32[5]{0:T(128)S(1)} %stack.31.refs_0_, f32[3,128,2048]{2,1,0:T(8,128)S(1)} %copy-done, f32[3,128,2048]{2,1,0:T(8,128)S(1)} %copy-done, f32[3,128,2048]{2,1,0:T(8,128)S(1)} %copy-done, bf16[512,256]{1,0:T(8,128)(2,1)S(1)} %copy-done.3, bf16[512,256]{1,0:T(8,128)(2,1)S(1)} %copy-done.2, ...), custom_call_target="tpu_custom_call" | custom-call | flops 603979776 | bytes 1572864 | tf_op jit(solution)/shard_map/along_x/pallas_call | solution.py:109
  6.3 1.5 %along_x.6 = (f32[6,32,512]{2,1,0:T(8,128)S(1)}, f32[6,32,512]{2,1,0:T(8,128)S(1)}, f32[6,32,512]{2,1,0:T(8,128)S(1)}, f32[6,32,512]{2,1,0:T(8,128)S(1)}) custom-call(s32[5]{0:T(128)S(1)} %stack.31.refs_0_, f32[3,128,2048]{2,1,0:T(8,128)S(1)} %copy-done, f32[3,128,2048]{2,1,0:T(8,128)S(1)} %copy-done, f32[3,128,2048]{2,1,0:T(8,128)S(1)} %copy-done, ...), custom_call_target="tpu_custom_call" | custom-call | flops 603979776 | bytes 3145728 | tf_op jit(solution)/shard_map/along_x/pallas_call | solution.py:109
  7.9 2.9 %collective-permute-start.4 = (f32[6,32,512]{2,1,0:T(8,128)S(1)}, f32[6,32,512]{2,1,0:T(8,128)S(1)}, u32[]{:S(2)}, u32[]{:S(2)}) collective-permute-start(f32[6,32,512]{2,1,0:T(8,128)S(1)} %get-tuple-element.23.refs_8_), channel_id=1, source_target_pairs={{0,8},{4,12},{8,0},{12,4},{16,24},{20,28},{24,16},{28,20},{1,9},{5... | collective-permute-start | bytes 1179656 | tf_op jit(solution)/shard_map/ppermute | solution.py:363
  10.8 1.5 %collective-permute-start.5 = (f32[6,32,512]{2,1,0:T(8,128)S(1)}, f32[6,32,512]{2,1,0:T(8,128)S(1)}, u32[]{:S(2)}, u32[]{:S(2)}) collective-permute-start(f32[6,32,512]{2,1,0:T(8,128)S(1)} %get-tuple-element.24.refs_9_), channel_id=1, source_target_pairs={{0,16},{4,20},{8,24},{12,28},{16,0},{20,4},{24,8},{28,12},{1,17},{... | collective-permute-start | bytes 1179656 | tf_op jit(solution)/shard_map/ppermute | solution.py:363
  12.6 1.5 %along_x.7.refs_6_.refs_2_ = f32[6,128,512]{2,1,0:T(8,128)S(1)} custom-call(s32[5]{0:T(128)S(1)} %stack.31.refs_0_, f32[3,128,2048]{2,1,0:T(8,128)S(1)} %copy-done, f32[3,128,2048]{2,1,0:T(8,128)S(1)} %copy-done, f32[3,128,2048]{2,1,0:T(8,128)S(1)} %copy-done, bf16[512,256]{1,0:T(8,128)(2,1)S(1)} %copy-done.3, bf16[512,256]{1,0:T(8,128)(2,1)S(1)} %copy-done.2, ...), custom_call_target="tpu_custom_call" | custom-call | flops 603979776 | bytes 3145728 | tf_op jit(solution)/shard_map/along_x/pallas_call | solution.py:109
  14.8 4.8 %collective-permute-start.2 = (f32[6,128,512]{2,1,0:T(8,128)S(1)}, f32[6,128,512]{2,1,0:T(8,128)S(1)}, u32[]{:S(2)}, u32[]{:S(2)}) collective-permute-start(f32[6,128,512]{2,1,0:T(8,128)S(1)} %along_x.7.refs_6_.refs_2_), channel_id=1, source_target_pairs={{0,1},{2,3},{1,0},{3,2},{4,5},{6,7},{5,4},{7,6},{8,9},{10,11},{9,8... | collective-permute-start | bytes 4718600 | tf_op jit(solution)/shard_map/ppermute | solution.py:353
  20.7 9.4 %collective-permute-done.5.refs_4_ = f32[6,32,512]{2,1,0:T(8,128)S(1)} collective-permute-done((f32[6,32,512]{2,1,0:T(8,128)S(1)}, f32[6,32,512]{2,1,0:T(8,128)S(1)}, u32[]{:S(2)}, u32[]{:S(2)}) %collective-permute-start.5) | collective-permute-done | bytes 393248 | tf_op jit(solution)/shard_map/ppermute | solution.py:363
  30.1 1.4 %along_z.2 = (f32[6,32,512]{2,1,0:T(8,128)S(1)}, f32[6,32,512]{2,1,0:T(8,128)S(1)}, f32[6,32,512]{2,1,0:T(8,128)S(1)}, f32[6,32,512]{2,1,0:T(8,128)S(1)}) custom-call(s32[5]{0:T(128)S(1)} %stack.31.refs_0_, bf16[384,192]{1,0:T(8,128)(2,1)S(1)} %pad_maximum_fusion.refs_1_, f32[6,32,512]{2,1,0:T(8,128)S(1)} %get-tuple-element.22.refs_7_.refs_2_, ...), custom_call_target="tpu_custom_call" | custom-call | flops 18119393280 | bytes 3145728 | tf_op jit(solution)/shard_map/along_z/pallas_call | solution.py:109
  33.7 1.4 %collective-permute-start.9 = (f32[6,32,512]{2,1,0:T(8,128)S(1)}, f32[6,32,512]{2,1,0:T(8,128)S(1)}, u32[]{:S(2)}, u32[]{:S(2)}) collective-permute-start(f32[6,32,512]{2,1,0:T(8,128)S(1)} %get-tuple-element.29), channel_id=1, source_target_pairs={{0,24},{4,28},{8,16},{12,20},{16,8},{20,12},{24,0},{28,4},{1,25},{... | collective-permute-start | bytes 1179656 | tf_op jit(solution)/shard_map/ppermute | solution.py:363
  35.1 8.6 %collective-permute-done.7.refs_2_ = f32[6,32,512]{2,1,0:T(8,128)S(1)} collective-permute-done((f32[6,32,512]{2,1,0:T(8,128)S(1)}, f32[6,32,512]{2,1,0:T(8,128)S(1)}, u32[]{:S(2)}, u32[]{:S(2)}) %collective-permute-start.7) | collective-permute-done | bytes 393248 | tf_op jit(solution)/shard_map/ppermute | solution.py:363
  43.7 7.7 %collective-permute-done.8.refs_3_ = f32[6,32,512]{2,1,0:T(8,128)S(1)} collective-permute-done((f32[6,32,512]{2,1,0:T(8,128)S(1)}, f32[6,32,512]{2,1,0:T(8,128)S(1)}, u32[]{:S(2)}, u32[]{:S(2)}) %collective-permute-start.8) | collective-permute-done | bytes 393248 | tf_op jit(solution)/shard_map/ppermute | solution.py:363
  53.0 4.4 %collective-permute-start.16 = (f32[6,128,512]{2,1,0:T(8,128)S(1)}, f32[6,128,512]{2,1,0:T(8,128)S(1)}, u32[]{:S(2)}, u32[]{:S(2)}) collective-permute-start(f32[6,128,512]{2,1,0:T(8,128)S(1)} %join.2.refs_5_.refs_2_), channel_id=1, source_target_pairs={{0,1},{2,3},{1,0},{3,2},{4,5},{6,7},{5,4},{7,6},{8,9},{10,11},{9,8... | collective-permute-start | bytes 4718600 | tf_op jit(solution)/shard_map/ppermute | solution.py:353
  57.3 2.8 %along_y.2 = (f32[6,32,512]{2,1,0:T(8,128)S(1)}, f32[6,32,512]{2,1,0:T(8,128)S(1)}, f32[6,32,512]{2,1,0:T(8,128)S(1)}, f32[6,32,512]{2,1,0:T(8,128)S(1)}) custom-call(s32[5]{0:T(128)S(1)} %stack.31.refs_0_, f32[6,128,512]{2,1,0:T(8,128)S(1)} %collective-permute-done.2.refs_1_, f32[6,128,512]{2,1,0:T(8,128)S(1)} %along_x.7.refs_6_.refs_2_, ...), custom_call_target="tpu_custom_call" | custom-call | flops 1207959552 | bytes 3145728 | tf_op jit(solution)/shard_map/along_y/pallas_call | solution.py:109
  62.2 1.5 %collective-permute-start.12 = (f32[6,32,512]{2,1,0:T(8,128)S(1)}, f32[6,32,512]{2,1,0:T(8,128)S(1)}, u32[]{:S(2)}, u32[]{:S(2)}) collective-permute-start(f32[6,32,512]{2,1,0:T(8,128)S(1)} %get-tuple-element.33), channel_id=1, source_target_pairs={{0,24},{4,28},{8,16},{12,20},{16,8},{20,12},{24,0},{28,4},{1,25},{... | collective-permute-start | bytes 1179656 | tf_op jit(solution)/shard_map/ppermute | solution.py:363
  63.7 8.6 %collective-permute-done.10.refs_3_ = f32[6,32,512]{2,1,0:T(8,128)S(1)} collective-permute-done((f32[6,32,512]{2,1,0:T(8,128)S(1)}, f32[6,32,512]{2,1,0:T(8,128)S(1)}, u32[]{:S(2)}, u32[]{:S(2)}) %collective-permute-start.10) | collective-permute-done | bytes 393248 | tf_op jit(solution)/shard_map/ppermute | solution.py:363
  72.3 5.0 %collective-permute-done.11.refs_4_ = f32[6,32,512]{2,1,0:T(8,128)S(1)} collective-permute-done((f32[6,32,512]{2,1,0:T(8,128)S(1)}, f32[6,32,512]{2,1,0:T(8,128)S(1)}, u32[]{:S(2)}, u32[]{:S(2)}) %collective-permute-start.11) | collective-permute-done | bytes 393248 | tf_op jit(solution)/shard_map/ppermute | solution.py:363
  77.3 1.4 %along_z.3 = (f32[6,32,512]{2,1,0:T(8,128)S(1)}, f32[6,32,512]{2,1,0:T(8,128)S(1)}, f32[6,32,512]{2,1,0:T(8,128)S(1)}, f32[6,32,512]{2,1,0:T(8,128)S(1)}) custom-call(s32[5]{0:T(128)S(1)} %stack.31.refs_0_, bf16[384,192]{1,0:T(8,128)(2,1)S(1)} %pad_maximum_fusion.refs_1_, f32[6,32,512]{2,1,0:T(8,128)S(1)} %get-tuple-element.30.refs_2_, ...), custom_call_target="tpu_custom_call" | custom-call | flops 603979776 | bytes 3145728 | tf_op jit(solution)/shard_map/along_z/pallas_call | solution.py:109
  78.7 1.5 %collective-permute-start.13 = (f32[6,32,512]{2,1,0:T(8,128)S(1)}, f32[6,32,512]{2,1,0:T(8,128)S(1)}, u32[]{:S(2)}, u32[]{:S(2)}) collective-permute-start(f32[6,32,512]{2,1,0:T(8,128)S(1)} %get-tuple-element.35.refs_6_), channel_id=1, source_target_pairs={{0,8},{4,12},{8,0},{12,4},{16,24},{20,28},{24,16},{28,20},{1,9},{5... | collective-permute-start | bytes 1179656 | tf_op jit(solution)/shard_map/ppermute | solution.py:363
  82.3 7.1 %collective-permute-done.16.refs_1_ = f32[6,128,512]{2,1,0:T(8,128)S(1)} collective-permute-done((f32[6,128,512]{2,1,0:T(8,128)S(1)}, f32[6,128,512]{2,1,0:T(8,128)S(1)}, u32[]{:S(2)}, u32[]{:S(2)}) %collective-permute-start.16) | collective-permute-done | bytes 1572896 | tf_op jit(solution)/shard_map/ppermute | solution.py:353
  89.4 1.7 %along_y.3 = f32[3,128,512]{2,1,0:T(8,128)S(1)} custom-call(s32[5]{0:T(128)S(1)} %stack.31.refs_0_, f32[6,128,512]{2,1,0:T(8,128)S(1)} %collective-permute-done.16.refs_1_, f32[6,128,512]{2,1,0:T(8,128)S(1)} %join.2.refs_5_.refs_2_, f32[6,128,512]{2,1,0:T(8,128)S(1)} %collective-permute-done.17.refs_3_, bf16[512,384]{1,0:T(8,128)(2,1)S(1)} %copy-done.4, ...), custom_call_target="tpu_custom_call" | custom-call | flops 603979776 | bytes 1572864 | tf_op jit(solution)/shard_map/along_y/pallas_call | solution.py:109
  91.3 3.4 %proximal.3 = (f32[3,128,2048]{2,1,0:T(8,128)}, f32[3,128,2048]{2,1,0:T(8,128)}) custom-call(s32[5]{0:T(128)S(1)} %stack.31.refs_0_, f32[6,128,512]{2,1,0:T(8,128)S(1)} %collective-permute-done.16.refs_1_, f32[6,128,512]{2,1,0:T(8,128)S(1)} %join.2.refs_5_.refs_2_, f32[6,128,512]{2,1,0:T(8,128)S(1)} %collective-permute-done.17.refs_3_, ...), custom_call_target="tpu_custom_call" | custom-call | flops 7864320 | bytes 12582912 | tf_op jit(solution)/shard_map/proximal/pallas_call | solution.py:109
  96.8 3.3 %proximal.4 = (f32[3,128,2048]{2,1,0:T(8,128)}, f32[3,128,2048]{2,1,0:T(8,128)}) custom-call(s32[5]{0:T(128)S(1)} %stack.31.refs_0_, f32[3,128,512]{2,1,0:T(8,128)S(1)} %collective-permute-done.19.refs_1_, f32[3,128,2048]{2,1,0:T(8,128)S(1)} %copy-done.1, ...), custom_call_target="tpu_custom_call", output_to_operand_aliasing={{0}: (8, {}), {1}: (9, {})} | custom-call | flops 15728640 | bytes 12582912 | tf_op jit(solution)/shard_map/proximal/pallas_call | solution.py:109
  100.1 2.2 %proximal.5 = (f32[3,128,2048]{2,1,0:T(8,128)}, f32[3,128,2048]{2,1,0:T(8,128)}) custom-call(s32[5]{0:T(128)S(1)} %stack.31.refs_0_, f32[3,128,512]{2,1,0:T(8,128)S(1)} %collective-permute-done.18.refs_1_, f32[3,128,2048]{2,1,0:T(8,128)S(1)} %copy-done.1, f32[3,128,2048]{2,1,0:T(8,128)} %get-tuple-element.40.refs_3_, ...), custom_call_target="tpu_custom_call", output_to_operand_aliasing={{0}: (3, {}), {1}: (4, {})} | custom-call | flops 7864320 | bytes 12582912 | tf_op jit(solution)/shard_map/proximal/pallas_call | solution.py:109
  (43 shorter events, 13.2 us)
Async XLA Ops:
  0.8 3.7 %copy-start = (f32[3,128,2048]{2,1,0:T(8,128)S(1)}, f32[3,128,2048]{2,1,0:T(8,128)}, u32[]{:S(2)}) copy-start(f32[3,128,2048]{2,1,0:T(8,128)} %refs_3_.7) | copy-start | bytes 9437188
  0.8 3.7 %copy-start.2 = (bf16[512,256]{1,0:T(8,128)(2,1)S(1)}, bf16[512,256]{1,0:T(8,128)(2,1)}, u32[]{:S(2)}) copy-start(bf16[512,256]{1,0:T(8,128)(2,1)} %constant.102.clone.refs_5_) | copy-start | bytes 786436
  0.8 3.7 %copy-start.3 = (bf16[512,256]{1,0:T(8,128)(2,1)S(1)}, bf16[512,256]{1,0:T(8,128)(2,1)}, u32[]{:S(2)}) copy-start(bf16[512,256]{1,0:T(8,128)(2,1)} %constant.101.clone.refs_4_) | copy-start | bytes 786436
  3.9 2.4 %collective-permute-start.1 = (f32[3,128,512]{2,1,0:T(8,128)S(1)}, f32[3,128,512]{2,1,0:T(8,128)S(1)}, u32[]{:S(2)}, u32[]{:S(2)}) collective-permute-start(f32[3,128,512]{2,1,0:T(8,128)S(1)} %along_x.4.refs_6_), channel_id=1, source_target_pairs={{0,4},{4,0},{8,12},{12,8},{16,20},{20,16},{24,28},{28,24},{1,5},{5... | collective-permute-start | bytes 2359304 | tf_op jit(solution)/shard_map/ppermute | solution.py:363
  5.9 6.7 %collective-permute-start = (f32[3,128,512]{2,1,0:T(8,128)S(1)}, f32[3,128,512]{2,1,0:T(8,128)S(1)}, u32[]{:S(2)}, u32[]{:S(2)}) collective-permute-start(f32[3,128,512]{2,1,0:T(8,128)S(1)} %along_x.5), channel_id=1, source_target_pairs={{0,4},{4,0},{8,12},{12,8},{16,20},{20,16},{24,28},{28,24},{1,5},{5... | collective-permute-start | bytes 2359304 | tf_op jit(solution)/shard_map/ppermute | solution.py:363
  7.9 12.8 %collective-permute-start.4 = (f32[6,32,512]{2,1,0:T(8,128)S(1)}, f32[6,32,512]{2,1,0:T(8,128)S(1)}, u32[]{:S(2)}, u32[]{:S(2)}) collective-permute-start(f32[6,32,512]{2,1,0:T(8,128)S(1)} %get-tuple-element.23.refs_8_), channel_id=1, source_target_pairs={{0,8},{4,12},{8,0},{12,4},{16,24},{20,28},{24,16},{28,20},{1,9},{5... | collective-permute-start | bytes 1179656 | tf_op jit(solution)/shard_map/ppermute | solution.py:363
  10.8 19.3 %collective-permute-start.5 = (f32[6,32,512]{2,1,0:T(8,128)S(1)}, f32[6,32,512]{2,1,0:T(8,128)S(1)}, u32[]{:S(2)}, u32[]{:S(2)}) collective-permute-start(f32[6,32,512]{2,1,0:T(8,128)S(1)} %get-tuple-element.24.refs_9_), channel_id=1, source_target_pairs={{0,16},{4,20},{8,24},{12,28},{16,0},{20,4},{24,8},{28,12},{1,17},{... | collective-permute-start | bytes 1179656 | tf_op jit(solution)/shard_map/ppermute | solution.py:363
  12.3 17.8 %collective-permute-start.6 = (f32[6,32,512]{2,1,0:T(8,128)S(1)}, f32[6,32,512]{2,1,0:T(8,128)S(1)}, u32[]{:S(2)}, u32[]{:S(2)}) collective-permute-start(f32[6,32,512]{2,1,0:T(8,128)S(1)} %get-tuple-element.25.refs_10_), channel_id=1, source_target_pairs={{0,24},{4,28},{8,16},{12,20},{16,8},{20,12},{24,0},{28,4},{1,25},{... | collective-permute-start | bytes 1179656 | tf_op jit(solution)/shard_map/ppermute | solution.py:363
  14.1 43.3 %collective-permute-start.3 = (f32[6,128,512]{2,1,0:T(8,128)S(1)}, f32[6,128,512]{2,1,0:T(8,128)S(1)}, u32[]{:S(2)}, u32[]{:S(2)}) collective-permute-start(f32[6,128,512]{2,1,0:T(8,128)S(1)} %along_x.7.refs_6_.refs_2_), channel_id=1, source_target_pairs={{1,2},{2,1},{5,6},{6,5},{9,10},{10,9},{13,14},{14,13},{17,18},{18,... | collective-permute-start | bytes 4718600 | tf_op jit(solution)/shard_map/ppermute | solution.py:353
  14.8 42.5 %collective-permute-start.2 = (f32[6,128,512]{2,1,0:T(8,128)S(1)}, f32[6,128,512]{2,1,0:T(8,128)S(1)}, u32[]{:S(2)}, u32[]{:S(2)}) collective-permute-start(f32[6,128,512]{2,1,0:T(8,128)S(1)} %along_x.7.refs_6_.refs_2_), channel_id=1, source_target_pairs={{0,1},{2,3},{1,0},{3,2},{4,5},{6,7},{5,4},{7,6},{8,9},{10,11},{9,8... | collective-permute-start | bytes 4718600 | tf_op jit(solution)/shard_map/ppermute | solution.py:353
  31.6 25.8 %copy-start.4 = (bf16[512,384]{1,0:T(8,128)(2,1)S(1)}, bf16[512,384]{1,0:T(8,128)(2,1)}, u32[]{:S(2)}) copy-start(bf16[512,384]{1,0:T(8,128)(2,1)} %constant.103.clone.refs_4_) | copy-start | bytes 1179652
  31.6 12.1 %collective-permute-start.7 = (f32[6,32,512]{2,1,0:T(8,128)S(1)}, f32[6,32,512]{2,1,0:T(8,128)S(1)}, u32[]{:S(2)}, u32[]{:S(2)}) collective-permute-start(f32[6,32,512]{2,1,0:T(8,128)S(1)} %get-tuple-element.27), channel_id=1, source_target_pairs={{0,8},{4,12},{8,0},{12,4},{16,24},{20,28},{24,16},{28,20},{1,9},{5... | collective-permute-start | bytes 1179656 | tf_op jit(solution)/shard_map/ppermute | solution.py:363
  32.9 18.5 %collective-permute-start.8 = (f32[6,32,512]{2,1,0:T(8,128)S(1)}, f32[6,32,512]{2,1,0:T(8,128)S(1)}, u32[]{:S(2)}, u32[]{:S(2)}) collective-permute-start(f32[6,32,512]{2,1,0:T(8,128)S(1)} %get-tuple-element.28), channel_id=1, source_target_pairs={{0,16},{4,20},{8,24},{12,28},{16,0},{20,4},{24,8},{28,12},{1,17},{... | collective-permute-start | bytes 1179656 | tf_op jit(solution)/shard_map/ppermute | solution.py:363
  33.7 17.7 %collective-permute-start.9 = (f32[6,32,512]{2,1,0:T(8,128)S(1)}, f32[6,32,512]{2,1,0:T(8,128)S(1)}, u32[]{:S(2)}, u32[]{:S(2)}) collective-permute-start(f32[6,32,512]{2,1,0:T(8,128)S(1)} %get-tuple-element.29), channel_id=1, source_target_pairs={{0,24},{4,28},{8,16},{12,20},{16,8},{20,12},{24,0},{28,4},{1,25},{... | collective-permute-start | bytes 1179656 | tf_op jit(solution)/shard_map/ppermute | solution.py:363
  52.0 30.3 %collective-permute-start.17 = (f32[6,128,512]{2,1,0:T(8,128)S(1)}, f32[6,128,512]{2,1,0:T(8,128)S(1)}, u32[]{:S(2)}, u32[]{:S(2)}) collective-permute-start(f32[6,128,512]{2,1,0:T(8,128)S(1)} %join.2.refs_5_.refs_2_), channel_id=1, source_target_pairs={{1,2},{2,1},{5,6},{6,5},{9,10},{10,9},{13,14},{14,13},{17,18},{18,... | collective-permute-start | bytes 4718600 | tf_op jit(solution)/shard_map/ppermute | solution.py:353
  53.0 36.4 %collective-permute-start.16 = (f32[6,128,512]{2,1,0:T(8,128)S(1)}, f32[6,128,512]{2,1,0:T(8,128)S(1)}, u32[]{:S(2)}, u32[]{:S(2)}) collective-permute-start(f32[6,128,512]{2,1,0:T(8,128)S(1)} %join.2.refs_5_.refs_2_), channel_id=1, source_target_pairs={{0,1},{2,3},{1,0},{3,2},{4,5},{6,7},{5,4},{7,6},{8,9},{10,11},{9,8... | collective-permute-start | bytes 4718600 | tf_op jit(solution)/shard_map/ppermute | solution.py:353
  60.2 12.1 %collective-permute-start.10 = (f32[6,32,512]{2,1,0:T(8,128)S(1)}, f32[6,32,512]{2,1,0:T(8,128)S(1)}, u32[]{:S(2)}, u32[]{:S(2)}) collective-permute-start(f32[6,32,512]{2,1,0:T(8,128)S(1)} %get-tuple-element.31), channel_id=1, source_target_pairs={{0,8},{4,12},{8,0},{12,4},{16,24},{20,28},{24,16},{28,20},{1,9},{5... | collective-permute-start | bytes 1179656 | tf_op jit(solution)/shard_map/ppermute | solution.py:363
  60.8 16.5 %collective-permute-start.11 = (f32[6,32,512]{2,1,0:T(8,128)S(1)}, f32[6,32,512]{2,1,0:T(8,128)S(1)}, u32[]{:S(2)}, u32[]{:S(2)}) collective-permute-start(f32[6,32,512]{2,1,0:T(8,128)S(1)} %get-tuple-element.32), channel_id=1, source_target_pairs={{0,16},{4,20},{8,24},{12,28},{16,0},{20,4},{24,8},{28,12},{1,17},{... | collective-permute-start | bytes 1179656 | tf_op jit(solution)/shard_map/ppermute | solution.py:363
  62.2 15.0 %collective-permute-start.12 = (f32[6,32,512]{2,1,0:T(8,128)S(1)}, f32[6,32,512]{2,1,0:T(8,128)S(1)}, u32[]{:S(2)}, u32[]{:S(2)}) collective-permute-start(f32[6,32,512]{2,1,0:T(8,128)S(1)} %get-tuple-element.33), channel_id=1, source_target_pairs={{0,24},{4,28},{8,16},{12,20},{16,8},{20,12},{24,0},{28,4},{1,25},{... | collective-permute-start | bytes 1179656 | tf_op jit(solution)/shard_map/ppermute | solution.py:363
  78.7 16.0 %collective-permute-start.13 = (f32[6,32,512]{2,1,0:T(8,128)S(1)}, f32[6,32,512]{2,1,0:T(8,128)S(1)}, u32[]{:S(2)}, u32[]{:S(2)}) collective-permute-start(f32[6,32,512]{2,1,0:T(8,128)S(1)} %get-tuple-element.35.refs_6_), channel_id=1, source_target_pairs={{0,8},{4,12},{8,0},{12,4},{16,24},{20,28},{24,16},{28,20},{1,9},{5... | collective-permute-start | bytes 1179656 | tf_op jit(solution)/shard_map/ppermute | solution.py:363
  80.2 15.9 %collective-permute-start.14 = (f32[6,32,512]{2,1,0:T(8,128)S(1)}, f32[6,32,512]{2,1,0:T(8,128)S(1)}, u32[]{:S(2)}, u32[]{:S(2)}) collective-permute-start(f32[6,32,512]{2,1,0:T(8,128)S(1)} %get-tuple-element.36.refs_7_), channel_id=1, source_target_pairs={{0,16},{4,20},{8,24},{12,28},{16,0},{20,4},{24,8},{28,12},{1,17},{... | collective-permute-start | bytes 1179656 | tf_op jit(solution)/shard_map/ppermute | solution.py:363
  80.9 15.2 %collective-permute-start.15 = (f32[6,32,512]{2,1,0:T(8,128)S(1)}, f32[6,32,512]{2,1,0:T(8,128)S(1)}, u32[]{:S(2)}, u32[]{:S(2)}) collective-permute-start(f32[6,32,512]{2,1,0:T(8,128)S(1)} %get-tuple-element.37.refs_8_), channel_id=1, source_target_pairs={{0,24},{4,28},{8,16},{12,20},{16,8},{20,12},{24,0},{28,4},{1,25},{... | collective-permute-start | bytes 1179656 | tf_op jit(solution)/shard_map/ppermute | solution.py:363
  91.1 5.7 %collective-permute-start.19 = (f32[3,128,512]{2,1,0:T(8,128)S(1)}, f32[3,128,512]{2,1,0:T(8,128)S(1)}, u32[]{:S(2)}, u32[]{:S(2)}) collective-permute-start(f32[3,128,512]{2,1,0:T(8,128)S(1)} %along_y.3), channel_id=1, source_target_pairs={{0,4},{4,0},{8,12},{12,8},{16,20},{20,16},{24,28},{28,24},{1,5},{5... | collective-permute-start | bytes 2359304 | tf_op jit(solution)/shard_map/ppermute | solution.py:363
  96.7 3.4 %collective-permute-start.18 = (f32[3,128,512]{2,1,0:T(8,128)S(1)}, f32[3,128,512]{2,1,0:T(8,128)S(1)}, u32[]{:S(2)}, u32[]{:S(2)}) collective-permute-start(f32[3,128,512]{2,1,0:T(8,128)S(1)} %join.3), channel_id=1, source_target_pairs={{0,4},{4,0},{8,12},{12,8},{16,20},{20,16},{24,28},{28,24},{1,5},{5... | collective-permute-start | bytes 2359304 | tf_op jit(solution)/shard_map/ppermute | solution.py:363
  (1 other events, 1.9 us)

commit v4 on v3

--- a/solution.py
+++ b/solution.py
@@ -38,7 +38,7 @@
 def y_table(rows):
     table = gauss(np.arange(rows + 2 * RADIUS)[None, :] - RADIUS - np.arange(rows)[:, None])
     before, own, behind = np.split(table, [RADIUS, RADIUS + rows], axis=1)
-    tables = [[behind, own, before], [before, own, behind]]
+    tables = [[before, own, behind], [behind, own, before]]
     return np.concatenate([term for blocks in tables for term in two_terms(np.concatenate(blocks, axis=1))], axis=0)
 
 
@@ -185,11 +185,11 @@
 
 
 def along_y(meta, cells, plane, table):
-    paired, own, other = cells
+    other, own, paired = cells
     cells = [
+        jnp.where(meta[2] == 1, -jnp.inf, other[plane]),
+        own[plane],
         jnp.where(meta[1] == 1, -jnp.inf, paired[plane]),
-        own[plane],
-        jnp.where(meta[2] == 1, -jnp.inf, other[plane]),
     ]
     return y_window(jnp.concatenate(cells, axis=0), table[...])
 
@@ -205,11 +205,11 @@
     return 12 * RADIUS * count, 4 * count
 
 
-def y_parts_kernel(meta, paired, own, other, table, *refs):
+def y_parts_kernel(meta, other, own, paired, table, *refs):
     outs, held = refs[:-1], refs[-1]
     planes, rows, width = own.shape
     for plane in range(planes):
-        held[plane] = along_y(meta, (paired, own, other), plane, table)
+        held[plane] = along_y(meta, (other, own, paired), plane, table)
     for out, (here, columns) in zip(outs, tiles(meta[0], outs, rows)):
         out[...] = held[:, here, columns]
 
@@ -222,9 +222,9 @@
     )
 
 
-def y_send_kernel(meta, paired, own, other, table, out):
+def y_send_kernel(meta, other, own, paired, table, out):
     for plane in range(out.shape[0]):
-        out[plane] = along_y(meta, (paired, own, other), plane, table)
+        out[plane] = along_y(meta, (other, own, paired), plane, table)
 
 
 def along_y_send(cells, meta, first, after=()):
@@ -350,7 +350,8 @@
 
 def neighbours(cells):
     count = lax.axis_size("gy")
-    return lax.ppermute(cells, "gy", pairs(count, 0)), cells, lax.ppermute(cells, "gy", pairs(count, 1))
+    paired = lax.ppermute(cells, "gy", pairs(count, 0))
+    return lax.ppermute(cells, "gy", pairs(count, 1)), cells, paired
 
 
 def row_meta():
@@ -432,7 +433,7 @@
     kernel = table(jnp.arange(2 * BLOCK) - depth, jnp.arange(BLOCK))
     logs = summed("...w,wo->...o", window, -1, kernel).reshape(potential.shape)
 
-    paired, _, other = neighbours(logs)
+    other, _, paired = neighbours(logs)
     up, down = jnp.where(position % 2 == 0, other, paired), jnp.where(position % 2 == 0, paired, other)
     up = jnp.where(position == 0, -jnp.inf, up[:, rows - depth :])
     down = jnp.where(position == devices - 1, -jnp.inf, down[:, :depth])

time: 103 us -> 102 us (level); the launches traced: 102 us -> 100 us
  starting transfers between devices: 26.8 us -> 21.3 us
  waiting for transfers between devices: 49.1 us -> 52.4 us
    ppermute x4, starting transfers between devices: 10.9 us -> 5.42 us  [the longest x2 3.74 us: neighbours(): paired = lax.ppermute(cells, 'gy', pairs(count, 0))]
    ppermute x16, waiting for transfers between devices: 41.9 us -> 46 us  [swap(): lax.ppermute(cells, 'gz', [(i, i ^ bits) for i in range(lax.axis_size('gz...]
  transfers between devices with their start and end apart: 20 -> 20, of which waited for: 9 -> 9; matrix products, arithmetic and copies ran while one was open for 0% -> 0% of each run, Pallas kernels for 19% -> 20%
where the time goes in v4:
time: 102 us; the launch traced here: 100 us
  waiting for transfers between devices  52.4 us (51%)
  Pallas kernels  25.1 us (25%)
  starting transfers between devices  21.3 us (21%)
  between operations  1.05 us (1%)
    ppermute x16, waiting for transfers between devices, swap(): lax.ppermute(cells, 'gz', [(i, i ^ bits) for i in range(lax.axis_size('gz...  46 us
    pallas_call x13, Pallas kernels, call(): pl.pallas_call(body, grid_spec=pltpu.PrefetchScalarGridSpec(num_scalar_pr...  25.1 us
    ppermute x16, starting transfers between devices, swap(): lax.ppermute(cells, 'gz', [(i, i ^ bits) for i in range(lax.axis_size('gz...  15.9 us
    ppermute x2, waiting for transfers between devices, neighbours(): paired = lax.ppermute(cells, 'gy', pairs(count, 0))  6.36 us
    ppermute x2, starting transfers between devices, neighbours(): paired = lax.ppermute(cells, 'gy', pairs(count, 0))  3.74 us
  transfers between devices with their start and end apart: 20, of which 9 were waited for; matrix products, arithmetic and copies ran while one was open for 0% of the time, Pallas kernels for 20%

profile of v4, /device:TPU:0, one launch (start us, length us, event | category | flops | bytes accessed | tf_op | source)
XLA Modules:
  0.0 100.3 jit_solution(18104285112750008673)
XLA Ops:
  0.8 3.1 %along_x.4.refs_6_ = f32[3,128,512]{2,1,0:T(8,128)S(1)} custom-call(s32[5]{0:T(128)S(1)} %stack.31.refs_0_, f32[3,128,2048]{2,1,0:T(8,128)} %refs_3_.7, f32[3,128,2048]{2,1,0:T(8,128)} %refs_3_.7, f32[3,128,2048]{2,1,0:T(8,128)} %refs_3_.7, bf16[512,256]{1,0:T(8,128)(2,1)} %constant.101.clone.refs_4_, bf16[512,256]{1,0:T(8,128)(2,1)} %constant.102.clone.refs_5_), custom_call_target="tpu_custom_call" | custom-call | flops 603979776 | bytes 1572864 | tf_op jit(solution)/shard_map/along_x/pallas_call | solution.py:109
  4.4 1.5 %along_x.5 = f32[3,128,512]{2,1,0:T(8,128)S(1)} custom-call(s32[5]{0:T(128)S(1)} %stack.31.refs_0_, f32[3,128,2048]{2,1,0:T(8,128)S(1)} %copy-done, f32[3,128,2048]{2,1,0:T(8,128)S(1)} %copy-done, f32[3,128,2048]{2,1,0:T(8,128)S(1)} %copy-done, bf16[512,256]{1,0:T(8,128)(2,1)S(1)} %copy-done.3, bf16[512,256]{1,0:T(8,128)(2,1)S(1)} %copy-done.2, ...), custom_call_target="tpu_custom_call" | custom-call | flops 603979776 | bytes 1572864 | tf_op jit(solution)/shard_map/along_x/pallas_call | solution.py:109
  6.3 1.5 %along_x.6 = (f32[6,32,512]{2,1,0:T(8,128)S(1)}, f32[6,32,512]{2,1,0:T(8,128)S(1)}, f32[6,32,512]{2,1,0:T(8,128)S(1)}, f32[6,32,512]{2,1,0:T(8,128)S(1)}) custom-call(s32[5]{0:T(128)S(1)} %stack.31.refs_0_, f32[3,128,2048]{2,1,0:T(8,128)S(1)} %copy-done, f32[3,128,2048]{2,1,0:T(8,128)S(1)} %copy-done, f32[3,128,2048]{2,1,0:T(8,128)S(1)} %copy-done, ...), custom_call_target="tpu_custom_call" | custom-call | flops 603979776 | bytes 3145728 | tf_op jit(solution)/shard_map/along_x/pallas_call | solution.py:109
  7.9 2.9 %collective-permute-start.4 = (f32[6,32,512]{2,1,0:T(8,128)S(1)}, f32[6,32,512]{2,1,0:T(8,128)S(1)}, u32[]{:S(2)}, u32[]{:S(2)}) collective-permute-start(f32[6,32,512]{2,1,0:T(8,128)S(1)} %get-tuple-element.23.refs_8_), channel_id=1, source_target_pairs={{0,8},{4,12},{8,0},{12,4},{16,24},{20,28},{24,16},{28,20},{1,9},{5... | collective-permute-start | bytes 1179656 | tf_op jit(solution)/shard_map/ppermute | solution.py:364
  10.8 1.5 %collective-permute-start.5 = (f32[6,32,512]{2,1,0:T(8,128)S(1)}, f32[6,32,512]{2,1,0:T(8,128)S(1)}, u32[]{:S(2)}, u32[]{:S(2)}) collective-permute-start(f32[6,32,512]{2,1,0:T(8,128)S(1)} %get-tuple-element.24.refs_9_), channel_id=1, source_target_pairs={{0,16},{4,20},{8,24},{12,28},{16,0},{20,4},{24,8},{28,12},{1,17},{... | collective-permute-start | bytes 1179656 | tf_op jit(solution)/shard_map/ppermute | solution.py:364
  12.6 1.5 %along_x.7.refs_6_.refs_2_ = f32[6,128,512]{2,1,0:T(8,128)S(1)} custom-call(s32[5]{0:T(128)S(1)} %stack.31.refs_0_, f32[3,128,2048]{2,1,0:T(8,128)S(1)} %copy-done, f32[3,128,2048]{2,1,0:T(8,128)S(1)} %copy-done, f32[3,128,2048]{2,1,0:T(8,128)S(1)} %copy-done, bf16[512,256]{1,0:T(8,128)(2,1)S(1)} %copy-done.3, bf16[512,256]{1,0:T(8,128)(2,1)S(1)} %copy-done.2, ...), custom_call_target="tpu_custom_call" | custom-call | flops 603979776 | bytes 3145728 | tf_op jit(solution)/shard_map/along_x/pallas_call | solution.py:109
  14.1 2.1 %collective-permute-start.3 = (f32[6,128,512]{2,1,0:T(8,128)S(1)}, f32[6,128,512]{2,1,0:T(8,128)S(1)}, u32[]{:S(2)}, u32[]{:S(2)}) collective-permute-start(f32[6,128,512]{2,1,0:T(8,128)S(1)} %along_x.7.refs_6_.refs_2_), channel_id=1, source_target_pairs={{0,1},{2,3},{1,0},{3,2},{4,5},{6,7},{5,4},{7,6},{8,9},{10,11},{9,8... | collective-permute-start | bytes 4718600 | tf_op jit(solution)/shard_map/ppermute | solution.py:353
  16.9 3.8 %collective-permute-done.4.refs_3_ = f32[6,32,512]{2,1,0:T(8,128)S(1)} collective-permute-done((f32[6,32,512]{2,1,0:T(8,128)S(1)}, f32[6,32,512]{2,1,0:T(8,128)S(1)}, u32[]{:S(2)}, u32[]{:S(2)}) %collective-permute-start.4) | collective-permute-done | bytes 393248 | tf_op jit(solution)/shard_map/ppermute | solution.py:364
  20.7 9.4 %collective-permute-done.5.refs_4_ = f32[6,32,512]{2,1,0:T(8,128)S(1)} collective-permute-done((f32[6,32,512]{2,1,0:T(8,128)S(1)}, f32[6,32,512]{2,1,0:T(8,128)S(1)}, u32[]{:S(2)}, u32[]{:S(2)}) %collective-permute-start.5) | collective-permute-done | bytes 393248 | tf_op jit(solution)/shard_map/ppermute | solution.py:364
  35.1 8.6 %collective-permute-done.7.refs_2_ = f32[6,32,512]{2,1,0:T(8,128)S(1)} collective-permute-done((f32[6,32,512]{2,1,0:T(8,128)S(1)}, f32[6,32,512]{2,1,0:T(8,128)S(1)}, u32[]{:S(2)}, u32[]{:S(2)}) %collective-permute-start.7) | collective-permute-done | bytes 393248 | tf_op jit(solution)/shard_map/ppermute | solution.py:364
  43.7 7.7 %collective-permute-done.8.refs_3_ = f32[6,32,512]{2,1,0:T(8,128)S(1)} collective-permute-done((f32[6,32,512]{2,1,0:T(8,128)S(1)}, f32[6,32,512]{2,1,0:T(8,128)S(1)}, u32[]{:S(2)}, u32[]{:S(2)}) %collective-permute-start.8) | collective-permute-done | bytes 393248 | tf_op jit(solution)/shard_map/ppermute | solution.py:364
  52.0 1.6 %collective-permute-start.17 = (f32[6,128,512]{2,1,0:T(8,128)S(1)}, f32[6,128,512]{2,1,0:T(8,128)S(1)}, u32[]{:S(2)}, u32[]{:S(2)}) collective-permute-start(f32[6,128,512]{2,1,0:T(8,128)S(1)} %join.2.refs_5_.refs_2_), channel_id=1, source_target_pairs={{0,1},{2,3},{1,0},{3,2},{4,5},{6,7},{5,4},{7,6},{8,9},{10,11},{9,8... | collective-permute-start | bytes 4718600 | tf_op jit(solution)/shard_map/ppermute | solution.py:353
  54.6 2.8 %along_y.2 = (f32[6,32,512]{2,1,0:T(8,128)S(1)}, f32[6,32,512]{2,1,0:T(8,128)S(1)}, f32[6,32,512]{2,1,0:T(8,128)S(1)}, f32[6,32,512]{2,1,0:T(8,128)S(1)}) custom-call(s32[5]{0:T(128)S(1)} %stack.31.refs_0_, f32[6,128,512]{2,1,0:T(8,128)S(1)} %collective-permute-done.2.refs_1_, f32[6,128,512]{2,1,0:T(8,128)S(1)} %along_x.7.refs_6_.refs_2_, ...), custom_call_target="tpu_custom_call" | custom-call | flops 1207959552 | bytes 3145728 | tf_op jit(solution)/shard_map/along_y/pallas_call | solution.py:109
  59.5 1.5 %collective-permute-start.12 = (f32[6,32,512]{2,1,0:T(8,128)S(1)}, f32[6,32,512]{2,1,0:T(8,128)S(1)}, u32[]{:S(2)}, u32[]{:S(2)}) collective-permute-start(f32[6,32,512]{2,1,0:T(8,128)S(1)} %get-tuple-element.33), channel_id=1, source_target_pairs={{0,24},{4,28},{8,16},{12,20},{16,8},{20,12},{24,0},{28,4},{1,25},{... | collective-permute-start | bytes 1179656 | tf_op jit(solution)/shard_map/ppermute | solution.py:364
  61.0 8.6 %collective-permute-done.10.refs_3_ = f32[6,32,512]{2,1,0:T(8,128)S(1)} collective-permute-done((f32[6,32,512]{2,1,0:T(8,128)S(1)}, f32[6,32,512]{2,1,0:T(8,128)S(1)}, u32[]{:S(2)}, u32[]{:S(2)}) %collective-permute-start.10) | collective-permute-done | bytes 393248 | tf_op jit(solution)/shard_map/ppermute | solution.py:364
  69.5 5.3 %collective-permute-done.11.refs_4_ = f32[6,32,512]{2,1,0:T(8,128)S(1)} collective-permute-done((f32[6,32,512]{2,1,0:T(8,128)S(1)}, f32[6,32,512]{2,1,0:T(8,128)S(1)}, u32[]{:S(2)}, u32[]{:S(2)}) %collective-permute-start.11) | collective-permute-done | bytes 393248 | tf_op jit(solution)/shard_map/ppermute | solution.py:364
  74.8 1.4 %along_z.3 = (f32[6,32,512]{2,1,0:T(8,128)S(1)}, f32[6,32,512]{2,1,0:T(8,128)S(1)}, f32[6,32,512]{2,1,0:T(8,128)S(1)}, f32[6,32,512]{2,1,0:T(8,128)S(1)}) custom-call(s32[5]{0:T(128)S(1)} %stack.31.refs_0_, bf16[384,192]{1,0:T(8,128)(2,1)S(1)} %pad_maximum_fusion.refs_1_, f32[6,32,512]{2,1,0:T(8,128)S(1)} %get-tuple-element.30.refs_2_, ...), custom_call_target="tpu_custom_call" | custom-call | flops 603979776 | bytes 3145728 | tf_op jit(solution)/shard_map/along_z/pallas_call | solution.py:109
  76.3 1.5 %collective-permute-start.13 = (f32[6,32,512]{2,1,0:T(8,128)S(1)}, f32[6,32,512]{2,1,0:T(8,128)S(1)}, u32[]{:S(2)}, u32[]{:S(2)}) collective-permute-start(f32[6,32,512]{2,1,0:T(8,128)S(1)} %get-tuple-element.35.refs_6_), channel_id=1, source_target_pairs={{0,8},{4,12},{8,0},{12,4},{16,24},{20,28},{24,16},{28,20},{1,9},{5... | collective-permute-start | bytes 1179656 | tf_op jit(solution)/shard_map/ppermute | solution.py:364
  79.8 6.4 %collective-permute-done.17.refs_3_ = f32[6,128,512]{2,1,0:T(8,128)S(1)} collective-permute-done((f32[6,128,512]{2,1,0:T(8,128)S(1)}, f32[6,128,512]{2,1,0:T(8,128)S(1)}, u32[]{:S(2)}, u32[]{:S(2)}) %collective-permute-start.17) | collective-permute-done | bytes 1572896 | tf_op jit(solution)/shard_map/ppermute | solution.py:353
  86.2 1.7 %along_y.3 = f32[3,128,512]{2,1,0:T(8,128)S(1)} custom-call(s32[5]{0:T(128)S(1)} %stack.31.refs_0_, f32[6,128,512]{2,1,0:T(8,128)S(1)} %collective-permute-done.16.refs_1_, f32[6,128,512]{2,1,0:T(8,128)S(1)} %join.2.refs_5_.refs_2_, f32[6,128,512]{2,1,0:T(8,128)S(1)} %collective-permute-done.17.refs_3_, bf16[512,384]{1,0:T(8,128)(2,1)S(1)} %copy-done.4, ...), custom_call_target="tpu_custom_call" | custom-call | flops 603979776 | bytes 1572864 | tf_op jit(solution)/shard_map/along_y/pallas_call | solution.py:109
  88.1 3.4 %proximal.3 = (f32[3,128,2048]{2,1,0:T(8,128)}, f32[3,128,2048]{2,1,0:T(8,128)}) custom-call(s32[5]{0:T(128)S(1)} %stack.31.refs_0_, f32[6,128,512]{2,1,0:T(8,128)S(1)} %collective-permute-done.16.refs_1_, f32[6,128,512]{2,1,0:T(8,128)S(1)} %join.2.refs_5_.refs_2_, f32[6,128,512]{2,1,0:T(8,128)S(1)} %collective-permute-done.17.refs_3_, ...), custom_call_target="tpu_custom_call" | custom-call | flops 7864320 | bytes 12582912 | tf_op jit(solution)/shard_map/proximal/pallas_call | solution.py:109
  91.5 2.5 %collective-permute-done.14.refs_3_.refs_5_ = f32[6,32,512]{2,1,0:T(8,128)S(1)} collective-permute-done((f32[6,32,512]{2,1,0:T(8,128)S(1)}, f32[6,32,512]{2,1,0:T(8,128)S(1)}, u32[]{:S(2)}, u32[]{:S(2)}) %collective-permute-start.14) | collective-permute-done | bytes 393248 | tf_op jit(solution)/shard_map/ppermute | solution.py:364
  94.6 3.3 %proximal.4 = (f32[3,128,2048]{2,1,0:T(8,128)}, f32[3,128,2048]{2,1,0:T(8,128)}) custom-call(s32[5]{0:T(128)S(1)} %stack.31.refs_0_, f32[3,128,512]{2,1,0:T(8,128)S(1)} %collective-permute-done.19.refs_1_, f32[3,128,2048]{2,1,0:T(8,128)S(1)} %copy-done.1, ...), custom_call_target="tpu_custom_call", output_to_operand_aliasing={{0}: (8, {}), {1}: (9, {})} | custom-call | flops 15728640 | bytes 12582912 | tf_op jit(solution)/shard_map/proximal/pallas_call | solution.py:109
  98.0 2.2 %proximal.5 = (f32[3,128,2048]{2,1,0:T(8,128)}, f32[3,128,2048]{2,1,0:T(8,128)}) custom-call(s32[5]{0:T(128)S(1)} %stack.31.refs_0_, f32[3,128,512]{2,1,0:T(8,128)S(1)} %collective-permute-done.18.refs_1_, f32[3,128,2048]{2,1,0:T(8,128)S(1)} %copy-done.1, f32[3,128,2048]{2,1,0:T(8,128)} %get-tuple-element.40.refs_3_, ...), custom_call_target="tpu_custom_call", output_to_operand_aliasing={{0}: (3, {}), {1}: (4, {})} | custom-call | flops 7864320 | bytes 12582912 | tf_op jit(solution)/shard_map/proximal/pallas_call | solution.py:109
  (43 shorter events, 13.6 us)
Async XLA Ops:
  0.8 3.7 %copy-start = (f32[3,128,2048]{2,1,0:T(8,128)S(1)}, f32[3,128,2048]{2,1,0:T(8,128)}, u32[]{:S(2)}) copy-start(f32[3,128,2048]{2,1,0:T(8,128)} %refs_3_.7) | copy-start | bytes 9437188
  0.8 3.7 %copy-start.2 = (bf16[512,256]{1,0:T(8,128)(2,1)S(1)}, bf16[512,256]{1,0:T(8,128)(2,1)}, u32[]{:S(2)}) copy-start(bf16[512,256]{1,0:T(8,128)(2,1)} %constant.102.clone.refs_5_) | copy-start | bytes 786436
  0.8 3.7 %copy-start.3 = (bf16[512,256]{1,0:T(8,128)(2,1)S(1)}, bf16[512,256]{1,0:T(8,128)(2,1)}, u32[]{:S(2)}) copy-start(bf16[512,256]{1,0:T(8,128)(2,1)} %constant.101.clone.refs_4_) | copy-start | bytes 786436
  3.9 2.4 %collective-permute-start.1 = (f32[3,128,512]{2,1,0:T(8,128)S(1)}, f32[3,128,512]{2,1,0:T(8,128)S(1)}, u32[]{:S(2)}, u32[]{:S(2)}) collective-permute-start(f32[3,128,512]{2,1,0:T(8,128)S(1)} %along_x.4.refs_6_), channel_id=1, source_target_pairs={{0,4},{4,0},{8,12},{12,8},{16,20},{20,16},{24,28},{28,24},{1,5},{5... | collective-permute-start | bytes 2359304 | tf_op jit(solution)/shard_map/ppermute | solution.py:364
  5.9 6.7 %collective-permute-start = (f32[3,128,512]{2,1,0:T(8,128)S(1)}, f32[3,128,512]{2,1,0:T(8,128)S(1)}, u32[]{:S(2)}, u32[]{:S(2)}) collective-permute-start(f32[3,128,512]{2,1,0:T(8,128)S(1)} %along_x.5), channel_id=1, source_target_pairs={{0,4},{4,0},{8,12},{12,8},{16,20},{20,16},{24,28},{28,24},{1,5},{5... | collective-permute-start | bytes 2359304 | tf_op jit(solution)/shard_map/ppermute | solution.py:364
  7.9 12.8 %collective-permute-start.4 = (f32[6,32,512]{2,1,0:T(8,128)S(1)}, f32[6,32,512]{2,1,0:T(8,128)S(1)}, u32[]{:S(2)}, u32[]{:S(2)}) collective-permute-start(f32[6,32,512]{2,1,0:T(8,128)S(1)} %get-tuple-element.23.refs_8_), channel_id=1, source_target_pairs={{0,8},{4,12},{8,0},{12,4},{16,24},{20,28},{24,16},{28,20},{1,9},{5... | collective-permute-start | bytes 1179656 | tf_op jit(solution)/shard_map/ppermute | solution.py:364
  10.8 19.3 %collective-permute-start.5 = (f32[6,32,512]{2,1,0:T(8,128)S(1)}, f32[6,32,512]{2,1,0:T(8,128)S(1)}, u32[]{:S(2)}, u32[]{:S(2)}) collective-permute-start(f32[6,32,512]{2,1,0:T(8,128)S(1)} %get-tuple-element.24.refs_9_), channel_id=1, source_target_pairs={{0,16},{4,20},{8,24},{12,28},{16,0},{20,4},{24,8},{28,12},{1,17},{... | collective-permute-start | bytes 1179656 | tf_op jit(solution)/shard_map/ppermute | solution.py:364
  12.3 17.8 %collective-permute-start.6 = (f32[6,32,512]{2,1,0:T(8,128)S(1)}, f32[6,32,512]{2,1,0:T(8,128)S(1)}, u32[]{:S(2)}, u32[]{:S(2)}) collective-permute-start(f32[6,32,512]{2,1,0:T(8,128)S(1)} %get-tuple-element.25.refs_10_), channel_id=1, source_target_pairs={{0,24},{4,28},{8,16},{12,20},{16,8},{20,12},{24,0},{28,4},{1,25},{... | collective-permute-start | bytes 1179656 | tf_op jit(solution)/shard_map/ppermute | solution.py:364
  14.1 40.5 %collective-permute-start.3 = (f32[6,128,512]{2,1,0:T(8,128)S(1)}, f32[6,128,512]{2,1,0:T(8,128)S(1)}, u32[]{:S(2)}, u32[]{:S(2)}) collective-permute-start(f32[6,128,512]{2,1,0:T(8,128)S(1)} %along_x.7.refs_6_.refs_2_), channel_id=1, source_target_pairs={{0,1},{2,3},{1,0},{3,2},{4,5},{6,7},{5,4},{7,6},{8,9},{10,11},{9,8... | collective-permute-start | bytes 4718600 | tf_op jit(solution)/shard_map/ppermute | solution.py:353
  16.2 38.4 %collective-permute-start.2 = (f32[6,128,512]{2,1,0:T(8,128)S(1)}, f32[6,128,512]{2,1,0:T(8,128)S(1)}, u32[]{:S(2)}, u32[]{:S(2)}) collective-permute-start(f32[6,128,512]{2,1,0:T(8,128)S(1)} %along_x.7.refs_6_.refs_2_), channel_id=1, source_target_pairs={{1,2},{2,1},{5,6},{6,5},{9,10},{10,9},{13,14},{14,13},{17,18},{18,... | collective-permute-start | bytes 4718600 | tf_op jit(solution)/shard_map/ppermute | solution.py:354
  31.6 23.1 %copy-start.4 = (bf16[512,384]{1,0:T(8,128)(2,1)S(1)}, bf16[512,384]{1,0:T(8,128)(2,1)}, u32[]{:S(2)}) copy-start(bf16[512,384]{1,0:T(8,128)(2,1)} %constant.103.clone.refs_4_) | copy-start | bytes 1179652
  31.6 12.1 %collective-permute-start.7 = (f32[6,32,512]{2,1,0:T(8,128)S(1)}, f32[6,32,512]{2,1,0:T(8,128)S(1)}, u32[]{:S(2)}, u32[]{:S(2)}) collective-permute-start(f32[6,32,512]{2,1,0:T(8,128)S(1)} %get-tuple-element.27), channel_id=1, source_target_pairs={{0,8},{4,12},{8,0},{12,4},{16,24},{20,28},{24,16},{28,20},{1,9},{5... | collective-permute-start | bytes 1179656 | tf_op jit(solution)/shard_map/ppermute | solution.py:364
  32.9 18.5 %collective-permute-start.8 = (f32[6,32,512]{2,1,0:T(8,128)S(1)}, f32[6,32,512]{2,1,0:T(8,128)S(1)}, u32[]{:S(2)}, u32[]{:S(2)}) collective-permute-start(f32[6,32,512]{2,1,0:T(8,128)S(1)} %get-tuple-element.28), channel_id=1, source_target_pairs={{0,16},{4,20},{8,24},{12,28},{16,0},{20,4},{24,8},{28,12},{1,17},{... | collective-permute-start | bytes 1179656 | tf_op jit(solution)/shard_map/ppermute | solution.py:364
  33.7 17.7 %collective-permute-start.9 = (f32[6,32,512]{2,1,0:T(8,128)S(1)}, f32[6,32,512]{2,1,0:T(8,128)S(1)}, u32[]{:S(2)}, u32[]{:S(2)}) collective-permute-start(f32[6,32,512]{2,1,0:T(8,128)S(1)} %get-tuple-element.29), channel_id=1, source_target_pairs={{0,24},{4,28},{8,16},{12,20},{16,8},{20,12},{24,0},{28,4},{1,25},{... | collective-permute-start | bytes 1179656 | tf_op jit(solution)/shard_map/ppermute | solution.py:364
  52.0 34.2 %collective-permute-start.17 = (f32[6,128,512]{2,1,0:T(8,128)S(1)}, f32[6,128,512]{2,1,0:T(8,128)S(1)}, u32[]{:S(2)}, u32[]{:S(2)}) collective-permute-start(f32[6,128,512]{2,1,0:T(8,128)S(1)} %join.2.refs_5_.refs_2_), channel_id=1, source_target_pairs={{0,1},{2,3},{1,0},{3,2},{4,5},{6,7},{5,4},{7,6},{8,9},{10,11},{9,8... | collective-permute-start | bytes 4718600 | tf_op jit(solution)/shard_map/ppermute | solution.py:353
  53.7 32.5 %collective-permute-start.16 = (f32[6,128,512]{2,1,0:T(8,128)S(1)}, f32[6,128,512]{2,1,0:T(8,128)S(1)}, u32[]{:S(2)}, u32[]{:S(2)}) collective-permute-start(f32[6,128,512]{2,1,0:T(8,128)S(1)} %join.2.refs_5_.refs_2_), channel_id=1, source_target_pairs={{1,2},{2,1},{5,6},{6,5},{9,10},{10,9},{13,14},{14,13},{17,18},{18,... | collective-permute-start | bytes 4718600 | tf_op jit(solution)/shard_map/ppermute | solution.py:354
  57.4 12.1 %collective-permute-start.10 = (f32[6,32,512]{2,1,0:T(8,128)S(1)}, f32[6,32,512]{2,1,0:T(8,128)S(1)}, u32[]{:S(2)}, u32[]{:S(2)}) collective-permute-start(f32[6,32,512]{2,1,0:T(8,128)S(1)} %get-tuple-element.31), channel_id=1, source_target_pairs={{0,8},{4,12},{8,0},{12,4},{16,24},{20,28},{24,16},{28,20},{1,9},{5... | collective-permute-start | bytes 1179656 | tf_op jit(solution)/shard_map/ppermute | solution.py:364
  58.1 16.7 %collective-permute-start.11 = (f32[6,32,512]{2,1,0:T(8,128)S(1)}, f32[6,32,512]{2,1,0:T(8,128)S(1)}, u32[]{:S(2)}, u32[]{:S(2)}) collective-permute-start(f32[6,32,512]{2,1,0:T(8,128)S(1)} %get-tuple-element.32), channel_id=1, source_target_pairs={{0,16},{4,20},{8,24},{12,28},{16,0},{20,4},{24,8},{28,12},{1,17},{... | collective-permute-start | bytes 1179656 | tf_op jit(solution)/shard_map/ppermute | solution.py:364
  59.5 15.3 %collective-permute-start.12 = (f32[6,32,512]{2,1,0:T(8,128)S(1)}, f32[6,32,512]{2,1,0:T(8,128)S(1)}, u32[]{:S(2)}, u32[]{:S(2)}) collective-permute-start(f32[6,32,512]{2,1,0:T(8,128)S(1)} %get-tuple-element.33), channel_id=1, source_target_pairs={{0,24},{4,28},{8,16},{12,20},{16,8},{20,12},{24,0},{28,4},{1,25},{... | collective-permute-start | bytes 1179656 | tf_op jit(solution)/shard_map/ppermute | solution.py:364
  76.3 15.2 %collective-permute-start.13 = (f32[6,32,512]{2,1,0:T(8,128)S(1)}, f32[6,32,512]{2,1,0:T(8,128)S(1)}, u32[]{:S(2)}, u32[]{:S(2)}) collective-permute-start(f32[6,32,512]{2,1,0:T(8,128)S(1)} %get-tuple-element.35.refs_6_), channel_id=1, source_target_pairs={{0,8},{4,12},{8,0},{12,4},{16,24},{20,28},{24,16},{28,20},{1,9},{5... | collective-permute-start | bytes 1179656 | tf_op jit(solution)/shard_map/ppermute | solution.py:364
  77.8 16.1 %collective-permute-start.14 = (f32[6,32,512]{2,1,0:T(8,128)S(1)}, f32[6,32,512]{2,1,0:T(8,128)S(1)}, u32[]{:S(2)}, u32[]{:S(2)}) collective-permute-start(f32[6,32,512]{2,1,0:T(8,128)S(1)} %get-tuple-element.36.refs_7_), channel_id=1, source_target_pairs={{0,16},{4,20},{8,24},{12,28},{16,0},{20,4},{24,8},{28,12},{1,17},{... | collective-permute-start | bytes 1179656 | tf_op jit(solution)/shard_map/ppermute | solution.py:364
  78.5 15.5 %collective-permute-start.15 = (f32[6,32,512]{2,1,0:T(8,128)S(1)}, f32[6,32,512]{2,1,0:T(8,128)S(1)}, u32[]{:S(2)}, u32[]{:S(2)}) collective-permute-start(f32[6,32,512]{2,1,0:T(8,128)S(1)} %get-tuple-element.37.refs_8_), channel_id=1, source_target_pairs={{0,24},{4,28},{8,16},{12,20},{16,8},{20,12},{24,0},{28,4},{1,25},{... | collective-permute-start | bytes 1179656 | tf_op jit(solution)/shard_map/ppermute | solution.py:364
  87.9 6.7 %collective-permute-start.19 = (f32[3,128,512]{2,1,0:T(8,128)S(1)}, f32[3,128,512]{2,1,0:T(8,128)S(1)}, u32[]{:S(2)}, u32[]{:S(2)}) collective-permute-start(f32[3,128,512]{2,1,0:T(8,128)S(1)} %along_y.3), channel_id=1, source_target_pairs={{0,4},{4,0},{8,12},{12,8},{16,20},{20,16},{24,28},{28,24},{1,5},{5... | collective-permute-start | bytes 2359304 | tf_op jit(solution)/shard_map/ppermute | solution.py:364
  94.5 3.4 %collective-permute-start.18 = (f32[3,128,512]{2,1,0:T(8,128)S(1)}, f32[3,128,512]{2,1,0:T(8,128)S(1)}, u32[]{:S(2)}, u32[]{:S(2)}) collective-permute-start(f32[3,128,512]{2,1,0:T(8,128)S(1)} %join.3), channel_id=1, source_target_pairs={{0,4},{4,0},{8,12},{12,8},{16,20},{20,16},{24,28},{28,24},{1,5},{5... | collective-permute-start | bytes 2359304 | tf_op jit(solution)/shard_map/ppermute | solution.py:364
  (1 other events, 1.9 us)
